TPU v7x, 128 devices: a whole 4x4x4 slice. The times are simulated.
128 devices in a mesh: fsdp: 128 (over y, z, x, core).
Axes of the slice: x: 4, y: 4, z: 4, core: 2. Of those that a mesh axis runs over, the one named last changes fastest.
Arguments:
- tokens: bfloat16 [16384, 2048], P('fsdp'), may hold values from -6 to 6
- cotangent: bfloat16 [16384, 2048], P('fsdp'), may hold values from -6 to 6
- attn_weight: float32 [2048, 8192], P('fsdp'), as said below
- mlp_weight: float32 [2048, 16896], P('fsdp'), as said below
- small_weight: float32 [7, 2048], P(None, 'fsdp'), as said below
- attn_first: float32 [2048, 8192], P('fsdp'), as said below
- attn_second: float32 [2048, 8192], P('fsdp'), as said below
- mlp_first: float32 [2048, 16896], P('fsdp'), as said below
- mlp_second: float32 [2048, 16896], P('fsdp'), as said below
- small_first: float32 [7, 2048], P(None, 'fsdp'), as said below
- small_second: float32 [7, 2048], P(None, 'fsdp'), as said below
Outputs:
- output: bfloat16 [16384, 2048], P('fsdp')
- grad_tokens: float32 [16384, 2048], P('fsdp')
- attn_new: float32 [2048, 8192], P('fsdp')
- attn_first_new: float32 [2048, 8192], P('fsdp')
- attn_second_new: float32 [2048, 8192], P('fsdp')
- mlp_new: float32 [2048, 16896], P('fsdp')
- mlp_first_new: float32 [2048, 16896], P('fsdp')
- mlp_second_new: float32 [2048, 16896], P('fsdp')
- small_new: float32 [7, 2048], P(None, 'fsdp')
- small_first_new: float32 [7, 2048], P(None, 'fsdp')
- small_second_new: float32 [7, 2048], P(None, 'fsdp')
Inputs may be any that keep to these rules, and one draw needn't show every extreme that they name: `attn_weight`: projection weights of order of one over the root of their fan-in. `mlp_weight`: projection weights of order of one over the root of their fan-in. `small_weight`: norm scales near one, biases small. `attn_first`: moments of a trainer's state. `attn_second`: positive. `mlp_first`: moments of a trainer's state. `mlp_second`: positive. `small_first`: moments of a trainer's state. `small_second`: positive.
All inputs are finite; a program needn't handle non-finite values.
Results may differ from a plain program's by a relative error of at most 0.012.
Values may be sent and summed in bfloat16 or wider, within the bound.
No kernel may reach another device: no remote copies, remote signals or barrier semaphores. Data moves between devices by JAX's collectives and lax.ppermute only.
A program may use at most 896 MiB of HBM per device.

v0:
```python
import jax
import jax.numpy as jnp
from jax import lax
from jax.sharding import PartitionSpec as P

HEAD = 64
ROT = 16
STEP = 10


norm_eps = 1e-05
mask_fill = -1000000000.0
rope_base = 10000.0
beta_one = 0.9
beta_two = 0.95
adam_eps = 1e-08
rate_matrix = 0.01
rate_small = 0.1
decay_matrix = 0.1


def rows_first(arrays, axis, dims):
    turned = [jnp.moveaxis(a, dim, 0) for a, dim in zip(arrays, dims)]
    both = jnp.concatenate([t.reshape(len(t), -1) for t in turned], axis=1)
    out, at, finished = (lax.all_gather(both, axis, axis=0, tiled=True), 0, [])
    for t, dim in zip(turned, dims):
        slab = out[:, at : at + t[0].size].reshape(-1, *t.shape[1:])
        finished.append(jnp.moveaxis(slab, 0, dim))
        at += t[0].size
    return tuple(finished)


def split_up(shard, dim, peers):
    before, after = (shard.shape[:dim], shard.shape[dim + 1 :])
    return jnp.moveaxis(shard.reshape(*before, peers, -1, *after), dim, 0)


def sum_packed(arrays, axis, dims):
    peers = lax.axis_size(axis)
    pieces = [split_up(a, dim, peers) for a, dim in zip(arrays, dims)]
    lines = jnp.concatenate([b.reshape(peers, -1) for b in pieces], axis=1)
    width = max(16, -(-lines.shape[1] // 1024) * 8)
    lines = jnp.pad(lines, ((0, 0), (0, width * 128 - lines.shape[1]))).reshape(-1, 128)
    vector, at, finished = (lax.psum_scatter(lines, axis, tiled=True).reshape(-1), 0, [])
    for b in pieces:
        part = b[0]
        finished.append(vector[at : at + part.size].reshape(part.shape))
        at += part.size
    return tuple(finished)


def product(left, right, dims):
    return lax.dot_general(left, right, (dims, ((), ())), preferred_element_type=jnp.float32)


def normalize(values):
    center = values - jnp.mean(values, axis=-1, keepdims=True)
    spread = jnp.mean(center * center, axis=-1, keepdims=True)
    scaled = lax.rsqrt(spread + norm_eps)
    return (center * scaled, scaled)


def norm_back(grad_normed, normal, scaled, gain):
    grad_hat = grad_normed * gain
    back = scaled * (
        grad_hat
        - jnp.mean(grad_hat, axis=-1, keepdims=True)
        - normal * jnp.mean(grad_hat * normal, axis=-1, keepdims=True)
    )
    return (back, jnp.sum(grad_normed * normal, axis=0), jnp.sum(grad_normed, axis=0))


def rope_tables(length):
    half = ROT // 2
    position = jnp.arange(length).astype(jnp.float32)
    inverse = rope_base ** (-(jnp.arange(half).astype(jnp.float32) * 2.0 / ROT))
    angle = position[:, None] * inverse[None, :]
    return (jnp.cos(angle), jnp.sin(angle))


def turn(tensor, cosine, sine, sign):
    half = ROT // 2
    first = tensor[..., :half]
    second = tensor[..., half:ROT]
    cos_b = cosine[:, None, :]
    sin_b = sine[:, None, :] * sign
    return jnp.concatenate(
        [first * cos_b - second * sin_b, second * cos_b + first * sin_b, tensor[..., ROT:]], axis=-1
    )


def attend_forward(query, keyed, valued):
    length = query.shape[0]
    block = min(512, length)
    factor = query.shape[-1] ** (-0.5)
    scores = jnp.einsum("qhe,khe->hqk", query, keyed, preferred_element_type=jnp.float32) * factor
    rows = 0 + jnp.arange(block)
    causal = rows[:, None] >= jnp.arange(length)[None, :]
    scores = jnp.where(causal[None], scores, mask_fill)
    top = jnp.max(scores, axis=-1, keepdims=True)
    weights = jnp.exp(scores - top)
    total = jnp.sum(weights, axis=-1, keepdims=True)
    prob_low = (weights / total).astype(jnp.bfloat16)
    outs = jnp.einsum("hqk,khe->qhe", prob_low, valued, preferred_element_type=jnp.float32)
    sums = top[..., 0] + jnp.log(total[..., 0])
    return (outs, sums)


def attend_backward(query, keyed, valued, grad_mixed, logsum):
    length = query.shape[0]
    block = min(512, length)
    factor = query.shape[-1] ** (-0.5)
    scores = jnp.einsum("qhe,khe->hqk", query, keyed, preferred_element_type=jnp.float32) * factor
    rows = 0 + jnp.arange(block)
    causal = rows[:, None] >= jnp.arange(length)[None, :]
    scores = jnp.where(causal[None], scores, mask_fill)
    prob = jnp.exp(scores - logsum[:, 0:block, None])
    prob_low = prob.astype(jnp.bfloat16)
    grad_value = jnp.einsum(
        "hqk,qhe->khe", prob_low, grad_mixed, preferred_element_type=jnp.float32
    )
    grad_prob = jnp.einsum("qhe,khe->hqk", grad_mixed, valued, preferred_element_type=jnp.float32)
    delta = jnp.sum(prob * grad_prob, axis=-1, keepdims=True)
    grad_scores = (prob * (grad_prob - delta)).astype(jnp.bfloat16)
    grad_query = (
        jnp.einsum("hqk,khe->qhe", grad_scores, keyed, preferred_element_type=jnp.float32) * factor
    )
    grad_key = (
        jnp.einsum("hqk,qhe->khe", grad_scores, query, preferred_element_type=jnp.float32) * factor
    )
    return (grad_query, grad_key, grad_value)


def adamw(weight, grad, first, second, rate, decay):
    first_new = beta_one * first + (1.0 - beta_one) * grad
    second_new = beta_two * second + (1.0 - beta_two) * grad * grad
    corr_one = 1.0 - beta_one**STEP
    corr_two = 1.0 - beta_two**STEP
    update = first_new / corr_one / (jnp.sqrt(second_new / corr_two) + adam_eps)
    return (weight - rate * (update + decay * weight), first_new, second_new)


def local(
    tokens,
    cotangent,
    attn_weight,
    mlp_weight,
    small_weight,
    attn_first,
    attn_second,
    mlp_first,
    mlp_second,
    small_first,
    small_second,
):
    length, width = tokens.shape
    hidden_width = mlp_weight.shape[1] // 3
    head_count = width // HEAD
    attn_full, small_full = rows_first(
        (attn_weight.astype(jnp.bfloat16), small_weight.astype(jnp.bfloat16)), "fsdp", (0, 1)
    )
    mlp_full = lax.all_gather(mlp_weight.astype(jnp.bfloat16), "fsdp", axis=0, tiled=True)
    params = small_full.astype(jnp.float32)
    inputs = tokens.astype(jnp.float32)
    normal_one, scaled_one = normalize(inputs)
    normed_low = (normal_one * params[0] + params[1]).astype(jnp.bfloat16)
    bias = jnp.concatenate([params[4], params[5], params[6]])
    projected = product(normed_low, attn_full[:, : 3 * width], ((1,), (0,))) + bias
    shaped = projected.reshape(length, 3, head_count, HEAD)
    cosine, sine = rope_tables(length)
    query_low = turn(shaped[:, 0], cosine, sine, 1.0).astype(jnp.bfloat16)
    key_low = turn(shaped[:, 1], cosine, sine, 1.0).astype(jnp.bfloat16)
    value_low = shaped[:, 2].astype(jnp.bfloat16)
    mixed, logsum = attend_forward(query_low, key_low, value_low)
    mixed_low = mixed.reshape(length, width).astype(jnp.bfloat16)
    residual = inputs + product(mixed_low, attn_full[:, 3 * width :], ((1,), (0,)))
    normal_two, scaled_two = normalize(residual)
    normed_two = (normal_two * params[2] + params[3]).astype(jnp.bfloat16)
    gate = product(normed_two, mlp_full[:, :hidden_width], ((1,), (0,)))
    upward = product(normed_two, mlp_full[:, hidden_width : 2 * hidden_width], ((1,), (0,)))
    sigma = jax.nn.sigmoid(gate)
    active = gate * sigma
    hidden_low = (active * upward).astype(jnp.bfloat16)
    output = residual + product(hidden_low, mlp_full[:, 2 * hidden_width :], ((1,), (1,)))
    mlp_back, params_back = (mlp_full, params)
    back_hidden = product(cotangent, mlp_back[:, 2 * hidden_width :], ((1,), (0,)))
    grad_gate_low = (back_hidden * upward * sigma * (1.0 + gate * (1.0 - sigma))).astype(
        jnp.bfloat16
    )
    grad_up_low = (back_hidden * active).astype(jnp.bfloat16)
    back_normed_two = product(grad_gate_low, mlp_back[:, :hidden_width], ((1,), (1,))) + product(
        grad_up_low, mlp_back[:, hidden_width : 2 * hidden_width], ((1,), (1,))
    )
    back_residual, gain_two_grad, shift_two_grad = norm_back(
        back_normed_two, normal_two, scaled_two, params_back[2]
    )
    back_residual = cotangent.astype(jnp.float32) + back_residual
    back_branch = back_residual.astype(jnp.bfloat16)
    grad_out_proj = product(mixed_low, back_branch, ((0,), (0,)))
    back_mixed = (
        product(back_branch, attn_full[:, 3 * width :], ((1,), (1,)))
        .astype(jnp.bfloat16)
        .reshape(length, head_count, HEAD)
    )
    back_query, back_key, back_value = attend_backward(
        query_low, key_low, value_low, back_mixed, logsum
    )
    back_query = turn(back_query, cosine, sine, -1.0)
    back_key = turn(back_key, cosine, sine, -1.0)
    back_proj = jnp.concatenate(
        [
            back_query.reshape(length, width),
            back_key.reshape(length, width),
            back_value.reshape(length, width),
        ],
        axis=1,
    ).astype(jnp.bfloat16)
    bias_grad = jnp.sum(back_proj, axis=0, dtype=jnp.float32)
    grad_qkv = product(normed_low, back_proj, ((0,), (0,)))
    back_normed_one = product(back_proj, attn_full[:, : 3 * width], ((1,), (1,)))
    back_inputs, gain_one_grad, shift_one_grad = norm_back(
        back_normed_one, normal_one, scaled_one, params_back[0]
    )
    grad_tokens = back_residual + back_inputs
    attn_term = jnp.concatenate([grad_qkv, grad_out_proj], axis=1)
    small_term = jnp.stack(
        [
            gain_one_grad,
            shift_one_grad,
            gain_two_grad,
            shift_two_grad,
            bias_grad[:width],
            bias_grad[width : 2 * width],
            bias_grad[2 * width :],
        ]
    )
    attn_grad, small_grad = sum_packed((attn_term, small_term), "fsdp", (0, 1))
    mlp_grad = lax.psum_scatter(
        jnp.concatenate(
            [
                product(normed_two, grad_gate_low, ((0,), (0,))),
                product(normed_two, grad_up_low, ((0,), (0,))),
                product(cotangent, hidden_low, ((0,), (0,))),
            ],
            axis=1,
        ),
        "fsdp",
        scatter_dimension=0,
        tiled=True,
    )
    attn_new, attn_first_new, attn_second_new = adamw(
        attn_weight, attn_grad, attn_first, attn_second, rate_matrix, decay_matrix
    )
    mlp_new, mlp_first_new, mlp_second_new = adamw(
        mlp_weight, mlp_grad, mlp_first, mlp_second, rate_matrix, decay_matrix
    )
    small_new, small_first_new, small_second_new = adamw(
        small_weight, small_grad, small_first, small_second, rate_small, 0.0
    )
    return (
        output.astype(jnp.bfloat16),
        grad_tokens,
        attn_new,
        attn_first_new,
        attn_second_new,
        mlp_new,
        mlp_first_new,
        mlp_second_new,
        small_new,
        small_first_new,
        small_second_new,
    )


def solution(mesh):
    placed = (
        P("fsdp", None),
        P("fsdp", None),
        P("fsdp", None),
        P("fsdp", None),
        P(None, "fsdp"),
        P("fsdp", None),
        P("fsdp", None),
        P("fsdp", None),
        P("fsdp", None),
        P(None, "fsdp"),
        P(None, "fsdp"),
    )
    return jax.shard_map(
        local,
        mesh=mesh,
        in_specs=placed,
        out_specs=(
            P("fsdp", None),
            P("fsdp", None),
            P("fsdp", None),
            P("fsdp", None),
            P("fsdp", None),
            P("fsdp", None),
            P("fsdp", None),
            P("fsdp", None),
            P(None, "fsdp"),
            P(None, "fsdp"),
            P(None, "fsdp"),
        ),
        check_vma=False,
    )
```

profile of v0, /device:TPU:18, one launch (start us, length us, event | category | flops | bytes accessed | tf_op | source)
XLA Modules:
  0.0 1652.4 jit_solution(1082411714163392726)
XLA Ops:
  13.9 107.2 %all-gather.3.cloned.1.call-done = bf16[2048,8199]{1,0:T(8,128)(2,1)} async-done(((bf16[16,8199]{1,0:T(8,128)(2,1)}), bf16[2048,8199]{1,0:T(8,128)(2,1)}) %all-gather.3.cloned.1.call-update) | async-done | bytes 33583120 | tf_op jit(solution)/shard_map/all_gather | solution.py:25
  126.2 12.1 fusion.20
  145.4 4.9 fusion.80
  151.6 140.7 %all-gather.5.cloned.1.call-done = bf16[2048,16896]{1,0:T(8,128)(2,1)} async-done(((bf16[16,16896]{1,0:T(8,128)(2,1)}), bf16[2048,16896]{1,0:T(8,128)(2,1)}) %all-gather.5.cloned.1.call-update) | async-done | bytes 69206032 | tf_op jit(solution)/shard_map/all_gather | solution.py:162
  292.3 9.5 fusion.4
  301.8 10.9 fusion.10
  312.8 12.3 multiply_convert_fusion.1
  325.1 13.7 fusion.8
  338.8 14.0 multiply_reduce_fusion.1
  355.6 7.1 fusion.36
  370.9 8.1 fusion.62
  379.9 20.9 %fusion.72 = f32[2048,6144]{1,0:T(8,128)} fusion(bf16[128,2048]{1,0:T(8,128)(2,1)S(1)} %copy-done.2, f32[2048]{0:T(1024)S(1)} %get-tuple-element.24, f32[2048]{0:T(1024)S(1)} %get-tuple-element.25, f32[128]{0:T(128)S(1)} %copy-done.51, f32[128]{0:T(128)S(1)} %copy-done.44, bf16[128,2048]{0,1:T(8,128)(2,1)S(1)} %bitcast.61, ...), kind=kOutput, calls=%fused_computation.151 | convolution fusion | flops 3227516928 | bytes 52446208 | tf_op jit(solution)/shard_map/dot_general | solution.py:53
  401.3 21.1 %fusion.56 = (f32[2048]{0:T(1024)S(1)}, f32[128]{0:T(128)}, f32[128]{0:T(128)}, f32[2048]{0:T(1024)S(1)}, f32[128,2048]{1,0:T(8,128)}) fusion(bf16[128,2048]{1,0:T(8,128)(2,1)S(1)} %copy-done.2, f32[128]{0:T(128)S(1)} %copy-done.51, f32[128]{0:T(128)S(1)} %copy-done.44, f32[2048]{0:T(1024)S(1)} %get-tuple-element.25, ...), kind=kOutput, calls=%fused_computation.70 | convolution fusion | flops 3228561408 | bytes 28338176 | tf_op jit(solution)/shard_map/dot_general | solution.py:53
  423.2 43.4 %pad_maximum_fusion.1 = f32[2048,8192]{1,0:T(8,128)} fusion(f32[2048,2048]{1,0:T(8,128)} %fusion.62, f32[2048,6144]{1,0:T(8,128)} %fusion.72), kind=kLoop, calls=%fused_computation.3 | loop fusion | flops 16777216 | bytes 134217728 | tf_op jit(solution)/shard_map/concatenate | solution.py:225
  466.6 47.5 %reshape_reshape.3 = f32[128,131072]{1,0:T(8,128)} reshape(f32[2048,8192]{1,0:T(8,128)} %pad_maximum_fusion.1) | data formatting | bytes 134217728 | tf_op jit(solution)/shard_map/reshape;reshape | solution.py:41
  514.1 44.6 %select_maximum_fusion = f32[128,132096]{1,0:T(8,128)} fusion(f32[128,112]{1,0:T(8,128)S(1)} %copy.60, f32[128,131072]{1,0:T(8,128)} %reshape_reshape.3), kind=kLoop, calls=%fused_computation.1 | loop fusion | flops 67633152 | bytes 134799360 | tf_op jit(solution)/shard_map/concatenate | solution.py:41
  558.7 77.4 %reshape.241 = f32[132096,128]{1,0:T(8,128)} reshape(f32[128,132096]{1,0:T(8,128)} %select_maximum_fusion) | data formatting | bytes 135266304 | tf_op jit(solution)/shard_map/reshape | solution.py:43
  637.6 20.6 %fusion.81 = f32[2048,5632]{1,0:T(8,128)} fusion(bf16[128,2048]{1,0:T(8,128)(2,1)S(1)} %copy-done.11, bf16[128,5632]{1,0:T(8,128)(2,1)S(1)} %copy-done.23), kind=kOutput, calls=%fused_computation.155 | convolution fusion | flops 2952790016 | bytes 48103424 | tf_op jit(solution)/shard_map/dot_general | solution.py:53
  658.2 21.4 %fusion.82 = f32[2048,5632]{1,0:T(8,128)} fusion(bf16[128,2048]{1,0:T(8,128)(2,1)S(1)} %copy-done.11, bf16[128,5632]{1,0:T(8,128)(2,1)S(1)} %copy-done.22), kind=kOutput, calls=%fused_computation.156 | convolution fusion | flops 2952790016 | bytes 48103424 | tf_op jit(solution)/shard_map/dot_general | solution.py:53
  679.7 20.0 %convolution_bitcast_fusion = f32[2048,5632]{1,0:T(8,128)} fusion(bf16[128,5632]{1,0:T(8,128)(2,1)S(1)} %copy-done.14, bf16[128,2048]{1,0:T(8,128)(2,1)S(1)} %copy-done.17), kind=kOutput, calls=%fused_computation.4 | convolution fusion | flops 2952790016 | bytes 48103424 | tf_op jit(solution)/shard_map/dot_general | solution.py:53
  699.7 96.3 %pad_maximum_fusion = f32[2048,16896]{1,0:T(8,128)} fusion(f32[2048,5632]{1,0:T(8,128)} %convolution_bitcast_fusion, f32[2048,5632]{1,0:T(8,128)} %fusion.82, f32[2048,5632]{1,0:T(8,128)} %fusion.81), kind=kLoop, calls=%fused_computation | loop fusion | flops 69206016 | bytes 276824064 | tf_op jit(solution)/shard_map/concatenate | solution.py:239
  800.2 13.3 fusion.33
  813.5 273.2 %all-reduce.4.cloned.1.call-done = f32[132096,128]{1,0:T(8,128)} async-done(((f32[132096,128]{1,0:T(8,128)}), f32[132096,128]{1,0:T(8,128)}) %all-reduce.4.cloned.1.call-update) | async-done | bytes 67633168
  1096.5 545.4 %reduce-scatter.2.cloned.1.call-done = f32[16,16896]{1,0:T(8,128)} async-done(((f32[2048,16896]{1,0:T(8,128)}), f32[16,16896]{1,0:T(8,128)}) %reduce-scatter.2.cloned.1.call-update) | async-done | bytes 1081360 | tf_op jit(solution)/shard_map/reduce_scatter | solution.py:238
  (210 shorter events, 51.8 us)
Async XLA Ops:
  7.2 113.9 %all-gather.3.cloned.1.call-start = ((), (), s32[]{:S(2)}) async-start(), calls=%async_computation.1 | async-start | bytes 34344960 | tf_op jit(solution)/shard_map/all_gather | solution.py:25
  9.9 282.4 %all-gather.5.cloned.1.call-start = ((), (), s32[]{:S(2)}) async-start(), calls=%async_computation.2 | async-start | bytes 69746688 | tf_op jit(solution)/shard_map/all_gather | solution.py:162
  12.1 1074.7 %all-reduce.4.cloned.1.call-start = ((), (), s32[]{:S(2)}) async-start(), calls=%async_computation.4 | async-start | bytes 135266304
  12.9 113.3 %copy-start.43 = (f32[128]{0:T(128)}, f32[128]{0:T(128)S(1)}, u32[]{:S(2)}) copy-start(f32[128]{0:T(128)S(1)} %broadcast_multiply_fusion.6) | copy-start | bytes 1540
  13.2 112.9 %copy-start.50 = (f32[128]{0:T(128)}, f32[128]{0:T(128)S(1)}, u32[]{:S(2)}) copy-start(f32[128]{0:T(128)S(1)} %add_rsqrt_fusion.1) | copy-start | bytes 1540
  126.2 275.1 %copy-start.27 = (f32[2048]{0:T(1024)}, f32[2048]{0:T(1024)S(1)}, u32[]{:S(2)}) copy-start(f32[2048]{0:T(1024)S(1)} %get-tuple-element.25) | copy-start | bytes 24580
  145.4 5.9 copy-start.38
  151.6 161.2 %copy-start.10 = (bf16[128,2048]{1,0:T(8,128)(2,1)}, bf16[128,2048]{1,0:T(8,128)(2,1)S(1)}, u32[]{:S(2)}) copy-start(bf16[128,2048]{1,0:T(8,128)(2,1)S(1)} %add_convert_fusion) | copy-start | bytes 1572868
  325.1 13.7 copy-start.21
  325.1 13.7 copy-start.8
  325.1 13.7 copy-start.39
  325.1 13.7 copy-start.56
  325.1 13.7 copy-start.60
  338.8 14.1 copy-start.16
  370.9 8.2 copy-start.41
  370.9 8.2 copy-start.46
  379.9 20.9 %copy-start.54 = (f32[2048]{0:T(1024)S(1)}, f32[2048]{0:T(1024)}, u32[]{:S(2)}) copy-start(f32[2048]{0:T(1024)} %get-tuple-element.11) | copy-start | bytes 24580
  379.9 21.1 %copy-start.53 = (f32[2048]{0:T(1024)S(1)}, f32[2048]{0:T(1024)}, u32[]{:S(2)}) copy-start(f32[2048]{0:T(1024)} %get-tuple-element.17) | copy-start | bytes 24580
  636.1 22.1 %copy-start.22 = (bf16[128,5632]{1,0:T(8,128)(2,1)S(1)}, bf16[128,5632]{1,0:T(8,128)(2,1)}, u32[]{:S(2)}) copy-start(bf16[128,5632]{1,0:T(8,128)(2,1)} %copy-done.21) | copy-start | bytes 4325380
  636.1 1005.7 %reduce-scatter.2.cloned.1.call-start = ((), (), s32[]{:S(2)}) async-start(), calls=%async_computation.3 | async-start | bytes 139493376 | tf_op jit(solution)/shard_map/reduce_scatter | solution.py:238
  658.2 21.5 %copy-start.14 = (bf16[128,5632]{1,0:T(8,128)(2,1)S(1)}, bf16[128,5632]{1,0:T(8,128)(2,1)}, u32[]{:S(2)}) copy-start(bf16[128,5632]{1,0:T(8,128)(2,1)} %get-tuple-element.37) | copy-start | bytes 4325380
  658.2 21.5 %copy-start.17 = (bf16[128,2048]{1,0:T(8,128)(2,1)S(1)}, bf16[128,2048]{1,0:T(8,128)(2,1)}, u32[]{:S(2)}) copy-start(bf16[128,2048]{1,0:T(8,128)(2,1)} %param.12) | copy-start | bytes 1572868
  1092.4 549.4 %copy-start.13 = (f32[16,16896]{1,0:T(8,128)S(1)}, f32[16,16896]{1,0:T(8,128)}, u32[]{:S(2)}) copy-start(f32[16,16896]{1,0:T(8,128)} %param.14) | copy-start | bytes 3244036
  1092.4 549.4 %copy-start.24 = (f32[16,16896]{1,0:T(8,128)S(1)}, f32[16,16896]{1,0:T(8,128)}, u32[]{:S(2)}) copy-start(f32[16,16896]{1,0:T(8,128)} %param.18) | copy-start | bytes 3244036
  (43 other events, 84.7 us)
Sparse Core Ops, SparseCore 0:
  11.6 109.5 all-gather.2
  124.7 167.5 all-gather.4
  636.2 450.4 all-reduce.3
  1093.5 548.2 reduce-scatter.1
where the time goes:
time: 1660 us; the launch traced here: 1650 us
  waiting for transfers between devices  1070 us (64%)
  matrix products  217 us (13%)
  other arithmetic  207 us (12%)
  local copies, waits for them, and re-layouts  146 us (9%)
    reduce_scatter x1, waiting for transfers between devices, local(): lax.psum_scatter(jnp.concatenate([product(normed_two, grad_gate_low, ((0,...  545 us
    unnamed x5, waiting for transfers between devices  273 us
    dot_general x15, matrix products, product(): lax.dot_general(left, right, (dims, ((), ())), preferred_element_type=jnp...  210 us
    all_gather x1, waiting for transfers between devices, local(): lax.all_gather(mlp_weight.astype(jnp.bfloat16), 'fsdp', axis=0, tiled=True)  141 us
    all_gather x1, waiting for transfers between devices, rows_first(): out, at, finished = (lax.all_gather(both, axis, axis=0, tiled=True), 0, [])  107 us
    concatenate x1, other arithmetic, local(): jnp.concatenate([product(normed_two, grad_gate_low, ((0,), (0,))), produc...  96.3 us
    reshape x1, local copies, waits for them, and re-layouts, sum_packed(): jnp.pad(lines, ((0, 0), (0, width * 128 - lines.shape[1]))).reshape(-1, 128)  77.4 us
    another operation x1, local copies, waits for them, and re-layouts, sum_packed(): lines = jnp.concatenate([b.reshape(peers, -1) for b in pieces], axis=1)  47.5 us
  transfers between devices with their start and end apart: 4, of which 4 were waited for; matrix products, arithmetic and copies ran while one was open for 13% of the time, Pallas kernels for 0%

commit v1 on v0

v1 whole, which is shorter than its diff:
```python
import jax
import jax.numpy as jnp
from jax import lax
from jax.sharding import Mesh, PartitionSpec as P

HEAD = 64
ROT = 16
STEP = 10

norm_eps = 1e-05
mask_fill = -1000000000.0
rope_base = 10000.0
beta_one = 0.9
beta_two = 0.95
adam_eps = 1e-08
rate_matrix = 0.01
rate_small = 0.1
decay_matrix = 0.1

LOW = jnp.bfloat16
FULL = jnp.float32

OUTER = ("y", "z")
GROUP = ("x", "core")
EVERY = OUTER + GROUP
RING = 4
MEMBERS = 8
OUTERS = 16


def product(left, right, dims):
    return lax.dot_general(left, right, (dims, ((), ())), preferred_element_type=FULL)


def normalize(values):
    center = values - jnp.mean(values, axis=-1, keepdims=True)
    spread = jnp.mean(center * center, axis=-1, keepdims=True)
    scaled = lax.rsqrt(spread + norm_eps)
    return (center * scaled, scaled)


def norm_back(grad_normed, normal, scaled, gain):
    grad_hat = grad_normed * gain
    back = scaled * (
        grad_hat
        - jnp.mean(grad_hat, axis=-1, keepdims=True)
        - normal * jnp.mean(grad_hat * normal, axis=-1, keepdims=True)
    )
    return (back, jnp.sum(grad_normed * normal, axis=0), jnp.sum(grad_normed, axis=0))


def rope_tables(length):
    half = ROT // 2
    position = jnp.arange(length).astype(FULL)
    inverse = rope_base ** (-(jnp.arange(half).astype(FULL) * 2.0 / ROT))
    angle = position[:, None] * inverse[None, :]
    return (jnp.cos(angle), jnp.sin(angle))


def turn(tensor, cosine, sine, sign):
    half = ROT // 2
    first = tensor[..., :half]
    second = tensor[..., half:ROT]
    cos_b = cosine[:, None, :]
    sin_b = sine[:, None, :] * sign
    return jnp.concatenate(
        [first * cos_b - second * sin_b, second * cos_b + first * sin_b, tensor[..., ROT:]], axis=-1
    )


def attend_forward(query, keyed, valued):
    length = query.shape[1]
    factor = query.shape[-1] ** (-0.5)
    scores = jnp.einsum("sqhe,skhe->shqk", query, keyed, preferred_element_type=FULL) * factor
    causal = jnp.arange(length)[:, None] >= jnp.arange(length)[None, :]
    scores = jnp.where(causal, scores, mask_fill)
    top = jnp.max(scores, axis=-1, keepdims=True)
    weights = jnp.exp(scores - top)
    total = jnp.sum(weights, axis=-1, keepdims=True)
    prob = weights / total
    prob_low = prob.astype(LOW)
    outs = jnp.einsum("shqk,skhe->sqhe", prob_low, valued, preferred_element_type=FULL)
    return (outs, prob)


def attend_backward(query, keyed, valued, grad_mixed, prob):
    factor = query.shape[-1] ** (-0.5)
    prob_low = prob.astype(LOW)
    grad_value = jnp.einsum("shqk,sqhe->skhe", prob_low, grad_mixed, preferred_element_type=FULL)
    grad_prob = jnp.einsum("sqhe,skhe->shqk", grad_mixed, valued, preferred_element_type=FULL)
    delta = jnp.sum(prob * grad_prob, axis=-1, keepdims=True)
    grad_scores = (prob * (grad_prob - delta)).astype(LOW)
    grad_query = (
        jnp.einsum("shqk,skhe->sqhe", grad_scores, keyed, preferred_element_type=FULL) * factor
    )
    grad_key = (
        jnp.einsum("shqk,sqhe->skhe", grad_scores, query, preferred_element_type=FULL) * factor
    )
    return (grad_query, grad_key, grad_value)


def adamw(weight, grad, first, second, rate, decay):
    first_new = beta_one * first + (1.0 - beta_one) * grad
    second_new = beta_two * second + (1.0 - beta_two) * grad * grad
    corr_one = 1.0 - beta_one**STEP
    corr_two = 1.0 - beta_two**STEP
    update = first_new / corr_one / (jnp.sqrt(second_new / corr_two) + adam_eps)
    return (weight - rate * (update + decay * weight), first_new, second_new)


def ring(values, hop):
    return lax.ppermute(values, "x", [(i, (i + hop) % RING) for i in range(RING)])


def sibling(values):
    return lax.ppermute(values, "core", [(0, 1), (1, 0)])


def gather_group(values):
    half = values.shape[0] // 2
    before = ring(values, 1)
    after = ring(values, -1)
    twin = sibling(values)
    far = jnp.concatenate([ring(before[:half], 1), ring(after[half:], -1)], axis=0)
    near = jnp.concatenate([before, after], axis=0)
    near_twin = sibling(near)
    far_twin = sibling(far)
    rows = values.shape[0]
    return jnp.concatenate(
        [values, twin, before, near_twin[:rows], after, near_twin[rows:], far, far_twin], axis=0
    )


def scatter_group(parts):
    rows = parts.shape[0] // MEMBERS
    half = rows // 2
    pieces = parts.reshape(RING, 2, rows, -1)
    mine, other = (pieces[:, 0], pieces[:, 1])
    far = mine[3].astype(FULL) + sibling(other[3]).astype(FULL)
    far = far.astype(LOW)
    up = ring(far[:half], 1)
    down = ring(far[half:], -1)
    both = sibling(other[:3]).astype(FULL) + mine[:3].astype(FULL)
    zero = jnp.zeros_like(up, dtype=FULL)
    to_after = (both[2] + jnp.concatenate([up.astype(FULL), zero], axis=0)).astype(LOW)
    to_before = (both[1] + jnp.concatenate([zero, down.astype(FULL)], axis=0)).astype(LOW)
    return both[0] + ring(to_after, 1).astype(FULL) + ring(to_before, -1).astype(FULL)


def block_moves(back):
    moves = []
    for outer in range(OUTERS):
        for member in range(MEMBERS):
            owner = member * OUTERS + outer
            here = outer * MEMBERS + member
            moves.append((here, owner) if back else (owner, here))
    return moves


def spread_columns(block, parts):
    rows = block.shape[0]
    return block.reshape(rows, parts, MEMBERS, -1).transpose(2, 0, 1, 3).reshape(MEMBERS, rows, -1)


def join_columns(pieces, parts):
    members, rows, width = pieces.shape
    turned = pieces.reshape(members, rows, parts, width // parts).transpose(1, 2, 0, 3)
    return turned.reshape(rows, members * width)


def local(
    tokens,
    cotangent,
    attn_weight,
    mlp_weight,
    small_weight,
    attn_first,
    attn_second,
    mlp_first,
    mlp_second,
    small_first,
    small_second,
):
    length, width = tokens.shape
    own_rows = attn_weight.shape[0]
    slab = own_rows * MEMBERS
    hidden = mlp_weight.shape[1] // 3 // MEMBERS
    inner = width // MEMBERS
    heads = inner // HEAD
    member = lax.axis_index(GROUP)

    attn_low = attn_weight.astype(LOW)
    small_low = jnp.pad(small_weight.astype(LOW).T, ((0, 0), (0, 121)))
    sent = jnp.concatenate(
        [spread_columns(attn_low[:, : 3 * width], 3), jnp.broadcast_to(small_low, (MEMBERS, own_rows, 128))],
        axis=2,
    )
    attn_slab = lax.all_to_all(sent, GROUP, 0, 0, tiled=True).reshape(slab, 3 * inner + 128)
    out_block = lax.ppermute(attn_low[:, 3 * width :], EVERY, block_moves(False))
    out_block = out_block.reshape(own_rows, MEMBERS, inner).transpose(1, 0, 2).reshape(slab, inner)
    attn_part = lax.all_gather(
        jnp.concatenate([attn_slab, out_block], axis=1), OUTER, axis=0, tiled=True
    )
    mlp_slab = lax.all_to_all(
        spread_columns(mlp_weight.astype(LOW), 3), GROUP, 0, 0, tiled=True
    ).reshape(slab, 3 * hidden)
    mlp_part = lax.all_gather(mlp_slab, OUTER, axis=0, tiled=True)
    weight_in = attn_part[:, : 3 * inner]
    params = attn_part[:, 3 * inner : 3 * inner + 7].T.astype(FULL)
    weight_out = (
        attn_part[:, 3 * inner + 128 :]
        .reshape(OUTERS, MEMBERS, own_rows, inner)
        .transpose(0, 2, 1, 3)
        .reshape(inner, width)
    )
    bias = lax.dynamic_slice_in_dim(params[4:7], member * inner, inner, axis=1).reshape(-1)
    weight_wide = mlp_part[:, : 2 * hidden]
    weight_down = mlp_part[:, 2 * hidden :]

    tokens_all = gather_group(tokens)
    cotangent_all = gather_group(cotangent)
    normal_all, _ = normalize(tokens_all.astype(FULL))
    normed_low = (normal_all * params[0] + params[1]).astype(LOW)
    projected = product(normed_low, weight_in, ((1,), (0,))) + bias
    shaped = projected.reshape(MEMBERS, length, 3, heads, HEAD)
    cosine, sine = rope_tables(length)
    query_low = turn(shaped[:, :, 0], cosine, sine, 1.0).astype(LOW)
    key_low = turn(shaped[:, :, 1], cosine, sine, 1.0).astype(LOW)
    value_low = shaped[:, :, 2].astype(LOW)
    mixed, prob = attend_forward(query_low, key_low, value_low)
    mixed_low = mixed.reshape(-1, inner).astype(LOW)
    inputs = tokens.astype(FULL)
    residual = inputs + scatter_group(product(mixed_low, weight_out, ((1,), (0,))).astype(LOW))

    normal_two, scaled_two = normalize(residual)
    normed_two = gather_group((normal_two * params[2] + params[3]).astype(LOW))
    both = product(normed_two, weight_wide, ((1,), (0,)))
    gate, upward = (both[:, :hidden], both[:, hidden:])
    sigma = jax.nn.sigmoid(gate)
    active = gate * sigma
    hidden_low = (active * upward).astype(LOW)
    back_hidden = product(cotangent_all, weight_down, ((1,), (0,)))
    back_wide = jnp.concatenate(
        [
            (back_hidden * upward * sigma * (1.0 + gate * (1.0 - sigma))).astype(LOW),
            (back_hidden * active).astype(LOW),
        ],
        axis=1,
    )
    back_normed_two = scatter_group(product(back_wide, weight_wide, ((1,), (1,))).astype(LOW))
    output = residual + scatter_group(product(hidden_low, weight_down, ((1,), (1,))).astype(LOW))
    mlp_grad = jnp.concatenate(
        [
            product(normed_two, back_wide, ((0,), (0,))).astype(LOW),
            product(cotangent_all, hidden_low, ((0,), (0,))).astype(LOW),
        ],
        axis=1,
    )
    mlp_grad = lax.psum_scatter(mlp_grad, OUTER, scatter_dimension=0, tiled=True)
    back_residual, gain_two_grad, shift_two_grad = norm_back(
        back_normed_two, normal_two, scaled_two, params[2]
    )
    back_residual = cotangent.astype(FULL) + back_residual

    back_branch = gather_group(back_residual.astype(LOW))
    grad_out = product(mixed_low, back_branch, ((0,), (0,)))
    back_mixed = (
        product(back_branch, weight_out, ((1,), (1,)))
        .astype(LOW)
        .reshape(MEMBERS, length, heads, HEAD)
    )
    back_query, back_key, back_value = attend_backward(
        query_low, key_low, value_low, back_mixed, prob
    )
    back_query = turn(back_query, cosine, sine, -1.0)
    back_key = turn(back_key, cosine, sine, -1.0)
    back_proj = jnp.concatenate(
        [
            back_query.reshape(-1, inner),
            back_key.reshape(-1, inner),
            back_value.reshape(-1, inner),
        ],
        axis=1,
    ).astype(LOW)
    bias_grad = jnp.sum(back_proj, axis=0, dtype=FULL)
    grad_in = product(normed_low, back_proj, ((0,), (0,)))
    back_normed_one = scatter_group(product(back_proj, weight_in, ((1,), (1,))).astype(LOW))
    normal_one, scaled_one = normalize(inputs)
    back_inputs, gain_one_grad, shift_one_grad = norm_back(
        back_normed_one, normal_one, scaled_one, params[0]
    )
    grad_tokens = back_residual + back_inputs

    norm_grads = jnp.stack([gain_one_grad, shift_one_grad, gain_two_grad, shift_two_grad], axis=1)
    bias_rows = jnp.pad(
        bias_grad.reshape(3, OUTERS, own_rows).transpose(1, 2, 0),
        ((0, 0), (0, slab - own_rows), (0, 0)),
    ).reshape(width, 3)
    small_rows = jnp.pad(jnp.concatenate([norm_grads, bias_rows], axis=1), ((0, 0), (0, 121)))
    grad_out = (
        grad_out.reshape(OUTERS, own_rows, MEMBERS, inner)
        .transpose(0, 2, 1, 3)
        .reshape(width, inner)
    )
    attn_grad = jnp.concatenate(
        [grad_in.astype(LOW), small_rows.astype(LOW), grad_out.astype(LOW)], axis=1
    )
    attn_grad = lax.psum_scatter(attn_grad, OUTER, scatter_dimension=0, tiled=True)
    out_grad = (
        attn_grad[:, 3 * inner + 128 :]
        .reshape(MEMBERS, own_rows, inner)
        .transpose(1, 0, 2)
        .reshape(own_rows, width)
    )
    bias_grad = attn_grad[:own_rows, 3 * inner : 3 * inner + 128]
    block = lax.ppermute(
        jnp.concatenate([out_grad, bias_grad], axis=1), EVERY, block_moves(True)
    ).astype(FULL)
    pieces = lax.all_to_all(
        attn_grad[:, : 3 * inner + 128].reshape(MEMBERS, own_rows, -1), GROUP, 0, 0, tiled=True
    ).astype(FULL)
    attn_grad = jnp.concatenate(
        [join_columns(pieces[:, :, : 3 * inner], 3), block[:, :width]], axis=1
    )
    norm_grads = jnp.sum(pieces[:, :, 3 * inner : 3 * inner + 4], axis=0)
    small_grad = jnp.concatenate([norm_grads, block[:, width + 4 : width + 7]], axis=1).T
    mlp_pieces = lax.all_to_all(
        mlp_grad.reshape(MEMBERS, own_rows, -1), GROUP, 0, 0, tiled=True
    ).astype(FULL)
    mlp_grad = join_columns(mlp_pieces, 3)

    attn_new, attn_first_new, attn_second_new = adamw(
        attn_weight, attn_grad, attn_first, attn_second, rate_matrix, decay_matrix
    )
    mlp_new, mlp_first_new, mlp_second_new = adamw(
        mlp_weight, mlp_grad, mlp_first, mlp_second, rate_matrix, decay_matrix
    )
    small_new, small_first_new, small_second_new = adamw(
        small_weight, small_grad, small_first, small_second, rate_small, 0.0
    )
    return (
        output.astype(LOW),
        grad_tokens,
        attn_new,
        attn_first_new,
        attn_second_new,
        mlp_new,
        mlp_first_new,
        mlp_second_new,
        small_new,
        small_first_new,
        small_second_new,
    )


def solution(mesh):
    grid = Mesh(mesh.devices.reshape(4, 4, 4, 2), EVERY)
    rows, columns = (P(EVERY, None), P(None, EVERY))
    return jax.shard_map(
        local,
        mesh=grid,
        in_specs=(rows,) * 4 + (columns,) + (rows,) * 4 + (columns,) * 2,
        out_specs=(rows,) * 8 + (columns,) * 3,
        check_vma=False,
    )
```

time: 1660 us -> 570 us (0.34)
  waiting for transfers between devices: 1070 us -> 239 us
  other arithmetic: 207 us -> 50.2 us
  matrix products: 217 us -> 73.9 us
  starting transfers between devices: 0.16 us -> 74.6 us
  local copies, waits for them, and re-layouts: 146 us -> 107 us
    reduce_scatter x1 -> x2, waiting for transfers between devices: 545 us -> 121 us  [the longest x1 71.8 us: local(): lax.psum_scatter(mlp_grad, OUTER, scatter_dimension=0, tiled=True)]
    unnamed x5 -> x4, waiting for transfers between devices: 273 us -> 0.07 us
    all_gather x2, waiting for transfers between devices: 248 us -> 0.02 us  [the longest x1 0.02 us: local(): lax.all_gather(jnp.concatenate([attn_slab, out_block], axis=1), OUTER, ax...]
    concatenate x5 -> x13, other arithmetic: 185 us -> 14 us  [the longest x1 4.16 us: local(): jnp.concatenate([product(normed_two, back_wide, ((0,), (0,))).astype(LOW)...]
    dot_general x21 -> x17, matrix products: 217 us -> 70.6 us  [the longest x12 64.1 us: product(): lax.dot_general(left, right, (dims, ((), ())), preferred_element_type=FULL)]
    ppermute x0 -> x54, waiting for transfers between devices: none -> 100 us  [the longest x32 93.9 us: ring(): lax.ppermute(values, 'x', [(i, (i + hop) % RING) for i in range(RING)])]
    reshape x3 -> x14, local copies, waits for them, and re-layouts: 77.6 us -> 17.1 us  [the longest x1 6.73 us: local(): shaped = projected.reshape(MEMBERS, length, 3, heads, HEAD)]
    ppermute x0 -> x54, starting transfers between devices: none -> 52.3 us  [the longest x32 38.3 us: ring(): lax.ppermute(values, 'x', [(i, (i + hop) % RING) for i in range(RING)])]
  transfers between devices with their start and end apart: 4 -> 62, of which waited for: 4 -> 30; matrix products, arithmetic and copies ran while one was open for 13% -> 28% of each run, Pallas kernels for 0% -> 0%
where the time goes in v1:
time: 570 us; the launch traced here: 560 us
  waiting for transfers between devices  239 us (42%)
  local copies, waits for them, and re-layouts  107 us (19%)
  starting transfers between devices  74.6 us (13%)
  matrix products  73.9 us (13%)
  other arithmetic  50.2 us (9%)
  between operations  15.8 us (3%)
    ppermute x32, waiting for transfers between devices, ring(): lax.ppermute(values, 'x', [(i, (i + hop) % RING) for i in range(RING)])  93.9 us
    reduce_scatter x1, waiting for transfers between devices, local(): lax.psum_scatter(mlp_grad, OUTER, scatter_dimension=0, tiled=True)  71.8 us
    dot_general x12, matrix products, product(): lax.dot_general(left, right, (dims, ((), ())), preferred_element_type=FULL)  64.1 us
    unnamed x176, local copies, waits for them, and re-layouts  57.2 us
    reduce_scatter x1, waiting for transfers between devices, local(): lax.psum_scatter(attn_grad, OUTER, scatter_dimension=0, tiled=True)  48.9 us
    ppermute x32, starting transfers between devices, ring(): lax.ppermute(values, 'x', [(i, (i + hop) % RING) for i in range(RING)])  38.3 us
  transfers between devices with their start and end apart: 62, of which 30 were waited for; matrix products, arithmetic and copies ran while one was open for 28% of the time, Pallas kernels for 0%

profile of v1, /device:TPU:18, one launch (start us, length us, event | category | flops | bytes accessed | tf_op | source)
XLA Modules:
  0.0 559.7 jit_solution(6519820346747923715)
XLA Ops:
  15.2 6.5 %collective-permute-start.7 = (bf16[16,2048]{1,0:T(8,128)(2,1)S(1)}, bf16[16,2048]{1,0:T(8,128)(2,1)S(1)}, u32[]{:S(2)}, u32[]{:S(2)}) collective-permute-start(bf16[16,2048]{1,0:T(8,128)(2,1)S(1)} %slice.416), channel_id=1, source_target_pairs={{0,0},{16,1},{32,2},{48,3},{64,4},{80,5},{96,6},{112,7},{1,8},{17,... | collective-permute-start | bytes 196616 | tf_op jit(solution)/shard_map/ppermute | solution.py:199
  35.2 6.7 %all-to-all-start.1 = ((bf16[8,16,2112]{2,1,0:T(8,128)(2,1)}), bf16[8,16,2112]{2,1,0:T(8,128)(2,1)S(1)}, u32[]{:S(2)}, u32[]{:S(2)}) async-start(bf16[8,16,2112]{2,1,0:T(8,128)(2,1)} %reshape.325), calls=%async_computation.1 | async-start | bytes 1114112 | tf_op jit(solution)/shard_map/all_to_all | solution.py:204
  49.3 9.8 %all-to-all-done.1 = bf16[8,16,2112]{2,1,0:T(8,128)(2,1)S(1)} async-done(((bf16[8,16,2112]{2,1,0:T(8,128)(2,1)}), bf16[8,16,2112]{2,1,0:T(8,128)(2,1)S(1)}, u32[]{:S(2)}, u32[]{:S(2)}) %all-to-all-start.1) | async-done | bytes 540704 | tf_op jit(solution)/shard_map/all_to_all | solution.py:204
  89.6 7.5 %fusion.26 = f32[1024,768]{1,0:T(8,128)} fusion(bf16[2048,1152]{1,0:T(8,128)(2,1)} %all-gather.3.cloned.1.call-done, f32[768]{0:T(1024)S(1)} %add.243, bf16[1024,2048]{1,0:T(8,128)(2,1)S(1)} %copy-done.1, f32[2048]{0:T(1024)S(1)} %get-tuple-element.32, f32[2048]{0:T(1024)S(1)} %get-tuple-element.33, f32[1024]{0:T(1024)S(1)} %add_rsqrt_fusion, ...), kind=kOutput, calls=%fused_computation.48 | convolution fusion | flops 3234594816 | bytes 10513408 | tf_op jit(solution)/shard_map/dot_general | solution.py:32
  97.1 6.7 %reshape.364 = f32[8,128,3,4,64]{4,3,2,1,0:T(4,128)} reshape(f32[1024,768]{1,0:T(8,128)} %fusion.26) | data formatting | bytes 6291456 | tf_op jit(solution)/shard_map/reshape | solution.py:225
  135.2 6.1 %collective-permute-done.10 = bf16[64,2048]{1,0:T(8,128)(2,1)S(1)} collective-permute-done((bf16[64,2048]{1,0:T(8,128)(2,1)S(1)}, bf16[64,2048]{1,0:T(8,128)(2,1)S(1)}, u32[]{:S(2)}, u32[]{:S(2)}) %collective-permute-start.10) | collective-permute-done | bytes 262176 | tf_op jit(solution)/shard_map/ppermute | solution.py:112
  145.7 10.0 %collective-permute-done.13 = bf16[128,2048]{1,0:T(8,128)(2,1)S(1)} collective-permute-done((bf16[128,2048]{1,0:T(8,128)(2,1)S(1)}, bf16[128,2048]{1,0:T(8,128)(2,1)S(1)}, u32[]{:S(2)}, u32[]{:S(2)}) %collective-permute-start.13) | collective-permute-done | bytes 524320 | tf_op jit(solution)/shard_map/ppermute | solution.py:112
  166.2 8.1 %collective-permute-done.15 = bf16[128,2048]{1,0:T(8,128)(2,1)S(1)} collective-permute-done((bf16[128,2048]{1,0:T(8,128)(2,1)S(1)}, bf16[128,2048]{1,0:T(8,128)(2,1)S(1)}, u32[]{:S(2)}, u32[]{:S(2)}) %collective-permute-start.15) | collective-permute-done | bytes 524320 | tf_op jit(solution)/shard_map/ppermute | solution.py:112
  192.9 10.6 %fusion.11 = f32[1024,1408]{1,0:T(8,128)S(1)} fusion(bf16[1024,2048]{1,0:T(8,128)(2,1)} %constant_dynamic-update-slice_fusion.7, bf16[2048,2112]{1,0:T(8,128)(2,1)} %all-gather.5.cloned.1.call-done), kind=kOutput, calls=%fused_computation.17 | convolution fusion | flops 5905580032 | bytes 15728640 | tf_op jit(solution)/shard_map/dot_general | solution.py:32
  207.8 6.9 %fusion.15 = bf16[1024,2048]{1,0:T(8,128)(2,1)S(1)} fusion(bf16[2048,2112]{1,0:T(8,128)(2,1)S(1)} %copy-done.55, bf16[1024,704]{1,0:T(8,128)(2,1)S(1)} %get-tuple-element.53, bf16[1024,704]{1,0:T(8,128)(2,1)S(1)} %get-tuple-element.52), kind=kOutput, calls=%fused_computation.21 | convolution fusion | flops 5913444352 | bytes 13107200 | tf_op jit(solution)/shard_map/dot_general | solution.py:32
  239.8 8.9 %collective-permute-done.39 = bf16[128,2048]{1,0:T(8,128)(2,1)S(1)} collective-permute-done((bf16[128,2048]{1,0:T(8,128)(2,1)S(1)}, bf16[128,2048]{1,0:T(8,128)(2,1)S(1)}, u32[]{:S(2)}, u32[]{:S(2)}) %collective-permute-start.39) | collective-permute-done | bytes 524320 | tf_op jit(solution)/shard_map/ppermute | solution.py:112
  248.7 10.4 %collective-permute-done.26 = bf16[128,2048]{1,0:T(8,128)(2,1)S(1)} collective-permute-done((bf16[128,2048]{1,0:T(8,128)(2,1)S(1)}, bf16[128,2048]{1,0:T(8,128)(2,1)S(1)}, u32[]{:S(2)}, u32[]{:S(2)}) %collective-permute-start.26) | collective-permute-done | bytes 524320 | tf_op jit(solution)/shard_map/ppermute | solution.py:112
  265.7 11.0 %collective-permute-done.41 = bf16[128,2048]{1,0:T(8,128)(2,1)S(1)} collective-permute-done((bf16[128,2048]{1,0:T(8,128)(2,1)S(1)}, bf16[128,2048]{1,0:T(8,128)(2,1)S(1)}, u32[]{:S(2)}, u32[]{:S(2)}) %collective-permute-start.41) | collective-permute-done | bytes 524320 | tf_op jit(solution)/shard_map/ppermute | solution.py:112
  281.6 6.5 %collective-permute-done.44 = bf16[64,2048]{1,0:T(8,128)(2,1)S(1)} collective-permute-done((bf16[64,2048]{1,0:T(8,128)(2,1)S(1)}, bf16[64,2048]{1,0:T(8,128)(2,1)S(1)}, u32[]{:S(2)}, u32[]{:S(2)}) %collective-permute-start.44) | collective-permute-done | bytes 262176 | tf_op jit(solution)/shard_map/ppermute | solution.py:112
  313.7 6.5 %copy.287 = bf16[2048,1024]{1,0:T(8,128)(2,1)} copy(bf16[2048,1024]{0,1:T(8,128)(2,1)} %bitcast.296) | data formatting | bytes 8388608 | tf_op jit(solution)/shard_map/dot_general | solution.py:32
  342.9 5.6 collective-permute-done.52
  354.9 6.7 %copy.305 = bf16[2048,1152]{1,0:T(8,128)(2,1)} copy(bf16[2048,1152]{0,1:T(8,128)(2,1)} %fusion.14) | data formatting | bytes 9437184
  363.0 5.5 convolution_convert_fusion.5
  368.6 9.8 %convolution_convert_fusion = bf16[2048,1408]{0,1:T(8,128)(2,1)S(1)} fusion(bf16[1024,2048]{1,0:T(8,128)(2,1)} %constant_dynamic-update-slice_fusion.7, bf16[1024,704]{1,0:T(8,128)(2,1)S(1)} %copy-done.61, bf16[1024,704]{1,0:T(8,128)(2,1)S(1)} %copy-done.59), kind=kOutput, calls=%fused_computation.14 | convolution fusion | flops 5914230784 | bytes 12845056 | tf_op jit(solution)/shard_map/dot_general | solution.py:32
  382.6 11.8 %copy.307 = bf16[2048,2112]{1,0:T(8,128)(2,1)} copy(bf16[2048,2112]{0,1:T(8,128)(2,1)} %pad_maximum_fusion) | data formatting | bytes 17301504
  394.4 48.9 %reduce-scatter.7.cloned.1.call-done = bf16[128,1152]{1,0:T(8,128)(2,1)} async-done(((bf16[2048,1152]{1,0:T(8,128)(2,1)}), bf16[128,1152]{1,0:T(8,128)(2,1)}) %reduce-scatter.7.cloned.1.call-update) | async-done | bytes 294928 | tf_op jit(solution)/shard_map/reduce_scatter | solution.py:308
  448.7 5.5 all-to-all-start.2
  460.6 71.8 %reduce-scatter.9.cloned.1.call-done = bf16[128,2112]{1,0:T(8,128)(2,1)} async-done(((bf16[2048,2112]{1,0:T(8,128)(2,1)}), bf16[128,2112]{1,0:T(8,128)(2,1)}) %reduce-scatter.9.cloned.1.call-update) | async-done | bytes 540688 | tf_op jit(solution)/shard_map/reduce_scatter | solution.py:259
  540.6 6.0 %all-to-all-done.3 = bf16[8,16,2112]{2,1,0:T(8,128)(2,1)S(1)} async-done(((bf16[8,16,2112]{2,1,0:T(8,128)(2,1)}), bf16[8,16,2112]{2,1,0:T(8,128)(2,1)S(1)}, u32[]{:S(2)}, u32[]{:S(2)}) %all-to-all-start.3) | async-done | bytes 540704 | tf_op jit(solution)/shard_map/all_to_all | solution.py:327
  (438 shorter events, 250.0 us)
Async XLA Ops:
  15.1 68.7 %all-gather.3.cloned.1.call-start = ((), (), s32[]{:S(2)}) async-start(), calls=%async_computation.6 | async-start | bytes 5013504 | tf_op jit(solution)/shard_map/all_gather | solution.py:201
  24.6 39.7 %collective-permute-start = (bf16[128,2048]{1,0:T(8,128)(2,1)S(1)}, bf16[128,2048]{1,0:T(8,128)(2,1)}, u32[]{:S(2)}, u32[]{:S(2)}) collective-permute-start(bf16[128,2048]{1,0:T(8,128)(2,1)S(1)} %copy-done.3), channel_id=1, source_target_pairs={{0,1},{1,0},{2,3},{3,2},{4,5},{5,4},{6,7},{7,6},{8,9},{9,8},{10,11... | collective-permute-start | bytes 1572872 | tf_op jit(solution)/shard_map/ppermute | solution.py:116
  24.9 21.2 %collective-permute-start.1 = (bf16[128,2048]{1,0:T(8,128)(2,1)S(1)}, bf16[128,2048]{1,0:T(8,128)(2,1)}, u32[]{:S(2)}, u32[]{:S(2)}) collective-permute-start(bf16[128,2048]{1,0:T(8,128)(2,1)S(1)} %copy-done.3), channel_id=1, source_target_pairs={{0,2},{2,4},{4,6},{6,0},{1,3},{3,5},{5,7},{7,1},{8,10},{10,12},{12... | collective-permute-start | bytes 1572872 | tf_op jit(solution)/shard_map/ppermute | solution.py:112
  27.0 19.3 %collective-permute-start.2 = (bf16[128,2048]{1,0:T(8,128)(2,1)S(1)}, bf16[128,2048]{1,0:T(8,128)(2,1)S(1)}, u32[]{:S(2)}, u32[]{:S(2)}) collective-permute-start(bf16[128,2048]{1,0:T(8,128)(2,1)S(1)} %copy-done.3), channel_id=1, source_target_pairs={{0,6},{2,0},{4,2},{6,4},{1,7},{3,1},{5,3},{7,5},{8,14},{10,8},{12,... | collective-permute-start | bytes 1572872 | tf_op jit(solution)/shard_map/ppermute | solution.py:112
  27.0 34.1 %collective-permute-start.28 = (bf16[128,2048]{1,0:T(8,128)(2,1)}, bf16[128,2048]{1,0:T(8,128)(2,1)S(1)}, u32[]{:S(2)}, u32[]{:S(2)}) collective-permute-start(bf16[128,2048]{1,0:T(8,128)(2,1)} %param.12), channel_id=1, source_target_pairs={{0,2},{2,4},{4,6},{6,0},{1,3},{3,5},{5,7},{7,1},{8,10},{10,12},{12... | collective-permute-start | bytes 1572872 | tf_op jit(solution)/shard_map/ppermute | solution.py:112
  29.0 32.2 %collective-permute-start.29 = (bf16[128,2048]{1,0:T(8,128)(2,1)}, bf16[128,2048]{1,0:T(8,128)(2,1)S(1)}, u32[]{:S(2)}, u32[]{:S(2)}) collective-permute-start(bf16[128,2048]{1,0:T(8,128)(2,1)} %param.12), channel_id=1, source_target_pairs={{0,6},{2,0},{4,2},{6,4},{1,7},{3,1},{5,3},{7,5},{8,14},{10,8},{12,... | collective-permute-start | bytes 1572872 | tf_op jit(solution)/shard_map/ppermute | solution.py:112
  35.2 23.9 %all-to-all-start.1 = ((bf16[8,16,2112]{2,1,0:T(8,128)(2,1)}), bf16[8,16,2112]{2,1,0:T(8,128)(2,1)S(1)}, u32[]{:S(2)}, u32[]{:S(2)}) async-start(bf16[8,16,2112]{2,1,0:T(8,128)(2,1)} %reshape.325), calls=%async_computation.1 | async-start | bytes 1114112 | tf_op jit(solution)/shard_map/all_to_all | solution.py:204
  41.9 151.0 %all-gather.5.cloned.1.call-start = ((), (), s32[]{:S(2)}) async-start(), calls=%async_computation.7 | async-start | bytes 9469952 | tf_op jit(solution)/shard_map/all_gather | solution.py:207
  46.1 80.9 %collective-permute-start.27 = (bf16[128,2048]{1,0:T(8,128)(2,1)}, bf16[128,2048]{1,0:T(8,128)(2,1)}, u32[]{:S(2)}, u32[]{:S(2)}) collective-permute-start(bf16[128,2048]{1,0:T(8,128)(2,1)} %param.12), channel_id=1, source_target_pairs={{0,1},{1,0},{2,3},{3,2},{4,5},{5,4},{6,7},{7,6},{8,9},{9,8},{10,11... | collective-permute-start | bytes 1572872 | tf_op jit(solution)/shard_map/ppermute | solution.py:116
  48.3 23.3 %collective-permute-start.3 = (bf16[256,2048]{1,0:T(8,128)(2,1)}, bf16[256,2048]{1,0:T(8,128)(2,1)}, u32[]{:S(2)}, u32[]{:S(2)}) collective-permute-start(bf16[256,2048]{1,0:T(8,128)(2,1)} %pad_maximum_fusion.4), channel_id=1, source_target_pairs={{0,1},{1,0},{2,3},{3,2},{4,5},{5,4},{6,7},{7,6},{8,9},{9,8},{10,11... | collective-permute-start | bytes 3145736 | tf_op jit(solution)/shard_map/ppermute | solution.py:116
  60.0 383.3 %reduce-scatter.7.cloned.1.call-start = ((), (), s32[]{:S(2)}) async-start(), calls=%async_computation.8 | async-start | bytes 5013504 | tf_op jit(solution)/shard_map/reduce_scatter | solution.py:308
  64.3 80.3 %collective-permute-start.30 = (bf16[256,2048]{1,0:T(8,128)(2,1)}, bf16[256,2048]{1,0:T(8,128)(2,1)}, u32[]{:S(2)}, u32[]{:S(2)}) collective-permute-start(bf16[256,2048]{1,0:T(8,128)(2,1)} %pad_maximum_fusion.6), channel_id=1, source_target_pairs={{0,1},{1,0},{2,3},{3,2},{4,5},{5,4},{6,7},{7,6},{8,9},{9,8},{10,11... | collective-permute-start | bytes 3145736 | tf_op jit(solution)/shard_map/ppermute | solution.py:116
  69.5 59.0 %collective-permute-start.31 = (bf16[64,2048]{1,0:T(8,128)(2,1)}, bf16[64,2048]{1,0:T(8,128)(2,1)}, u32[]{:S(2)}, u32[]{:S(2)}) collective-permute-start(bf16[64,2048]{1,0:T(8,128)(2,1)} %slice.462), channel_id=1, source_target_pairs={{0,2},{2,4},{4,6},{6,0},{1,3},{3,5},{5,7},{7,1},{8,10},{10,12},{12... | collective-permute-start | bytes 786440 | tf_op jit(solution)/shard_map/ppermute | solution.py:112
  69.6 58.9 %collective-permute-start.32 = (bf16[64,2048]{1,0:T(8,128)(2,1)}, bf16[64,2048]{1,0:T(8,128)(2,1)}, u32[]{:S(2)}, u32[]{:S(2)}) collective-permute-start(bf16[64,2048]{1,0:T(8,128)(2,1)} %slice.463), channel_id=1, source_target_pairs={{0,6},{2,0},{4,2},{6,4},{1,7},{3,1},{5,3},{7,5},{8,14},{10,8},{12,... | collective-permute-start | bytes 786440 | tf_op jit(solution)/shard_map/ppermute | solution.py:112
  129.6 45.8 %collective-permute-start.33 = (bf16[128,2048]{1,0:T(8,128)(2,1)S(1)}, bf16[128,2048]{1,0:T(8,128)(2,1)S(1)}, u32[]{:S(2)}, u32[]{:S(2)}) collective-permute-start(bf16[128,2048]{1,0:T(8,128)(2,1)S(1)} %pad_maximum_fusion.12), channel_id=1, source_target_pairs={{0,1},{1,0},{2,3},{3,2},{4,5},{5,4},{6,7},{7,6},{8,9},{9,8},{10,11... | collective-permute-start | bytes 1572872 | tf_op jit(solution)/shard_map/ppermute | solution.py:116
  220.0 14.2 %collective-permute-start.21 = (bf16[3,128,2048]{2,1,0:T(8,128)(2,1)S(1)}, bf16[3,128,2048]{2,1,0:T(8,128)(2,1)S(1)}, u32[]{:S(2)}, u32[]{:S(2)}) collective-permute-start(bf16[3,128,2048]{2,1,0:T(8,128)(2,1)S(1)} %slice_bitcast_fusion.5), channel_id=1, source_target_pairs={{0,1},{1,0},{2,3},{3,2},{4,5},{5,4},{6,7},{7,6},{8,9},{9,8},{10,11... | collective-permute-start | bytes 4718600 | tf_op jit(solution)/shard_map/ppermute | solution.py:116
  232.0 16.7 %collective-permute-start.39 = (bf16[128,2048]{1,0:T(8,128)(2,1)S(1)}, bf16[128,2048]{1,0:T(8,128)(2,1)S(1)}, u32[]{:S(2)}, u32[]{:S(2)}) collective-permute-start(bf16[128,2048]{1,0:T(8,128)(2,1)S(1)} %get-tuple-element.60), channel_id=1, source_target_pairs={{0,6},{2,0},{4,2},{6,4},{1,7},{3,1},{5,3},{7,5},{8,14},{10,8},{12,... | collective-permute-start | bytes 1572872 | tf_op jit(solution)/shard_map/ppermute | solution.py:112
  232.4 16.3 %collective-permute-start.37 = (bf16[128,2048]{1,0:T(8,128)(2,1)S(1)}, bf16[128,2048]{1,0:T(8,128)(2,1)S(1)}, u32[]{:S(2)}, u32[]{:S(2)}) collective-permute-start(bf16[128,2048]{1,0:T(8,128)(2,1)S(1)} %get-tuple-element.59), channel_id=1, source_target_pairs={{0,2},{2,4},{4,6},{6,0},{1,3},{3,5},{5,7},{7,1},{8,10},{10,12},{12... | collective-permute-start | bytes 1572872 | tf_op jit(solution)/shard_map/ppermute | solution.py:112
  237.7 21.4 %collective-permute-start.26 = (bf16[128,2048]{1,0:T(8,128)(2,1)S(1)}, bf16[128,2048]{1,0:T(8,128)(2,1)S(1)}, u32[]{:S(2)}, u32[]{:S(2)}) collective-permute-start(bf16[128,2048]{1,0:T(8,128)(2,1)S(1)} %get-tuple-element.62), channel_id=1, source_target_pairs={{0,6},{2,0},{4,2},{6,4},{1,7},{3,1},{5,3},{7,5},{8,14},{10,8},{12,... | collective-permute-start | bytes 1572872 | tf_op jit(solution)/shard_map/ppermute | solution.py:112
  238.0 21.1 %collective-permute-start.24 = (bf16[128,2048]{1,0:T(8,128)(2,1)S(1)}, bf16[128,2048]{1,0:T(8,128)(2,1)S(1)}, u32[]{:S(2)}, u32[]{:S(2)}) collective-permute-start(bf16[128,2048]{1,0:T(8,128)(2,1)S(1)} %get-tuple-element.61), channel_id=1, source_target_pairs={{0,2},{2,4},{4,6},{6,0},{1,3},{3,5},{5,7},{7,1},{8,10},{10,12},{12... | collective-permute-start | bytes 1572872 | tf_op jit(solution)/shard_map/ppermute | solution.py:112
  265.7 15.8 %collective-permute-start.40 = (bf16[128,2048]{1,0:T(8,128)(2,1)S(1)}, bf16[128,2048]{1,0:T(8,128)(2,1)S(1)}, u32[]{:S(2)}, u32[]{:S(2)}) collective-permute-start(bf16[128,2048]{1,0:T(8,128)(2,1)S(1)} %get-tuple-element.45), channel_id=1, source_target_pairs={{0,1},{1,0},{2,3},{3,2},{4,5},{5,4},{6,7},{7,6},{8,9},{9,8},{10,11... | collective-permute-start | bytes 1572872 | tf_op jit(solution)/shard_map/ppermute | solution.py:116
  312.8 15.2 %collective-permute-start.47 = (bf16[3,128,2048]{2,1,0:T(8,128)(2,1)}, bf16[3,128,2048]{2,1,0:T(8,128)(2,1)}, u32[]{:S(2)}, u32[]{:S(2)}) collective-permute-start(bf16[3,128,2048]{2,1,0:T(8,128)(2,1)} %slice_bitcast_fusion.1), channel_id=1, source_target_pairs={{0,1},{1,0},{2,3},{3,2},{4,5},{5,4},{6,7},{7,6},{8,9},{9,8},{10,11... | collective-permute-start | bytes 4718600 | tf_op jit(solution)/shard_map/ppermute | solution.py:116
  361.6 170.7 %reduce-scatter.9.cloned.1.call-start = ((), (), s32[]{:S(2)}) async-start(), calls=%async_computation.9 | async-start | bytes 9469952 | tf_op jit(solution)/shard_map/reduce_scatter | solution.py:259
  532.4 14.2 %all-to-all-start.3 = ((bf16[8,16,2112]{2,1,0:T(8,128)(2,1)}), bf16[8,16,2112]{2,1,0:T(8,128)(2,1)S(1)}, u32[]{:S(2)}, u32[]{:S(2)}) async-start(bf16[8,16,2112]{2,1,0:T(8,128)(2,1)} %bitcast.331), calls=%async_computation.3 | async-start | bytes 1114112 | tf_op jit(solution)/shard_map/all_to_all | solution.py:327
  (102 other events, 1286.8 us)
Sparse Core Ops, SparseCore 0:
  24.7 58.0 all-gather.2
  85.6 72.8 all-gather.4
  361.8 81.5 reduce-scatter.6
  446.6 85.7 reduce-scatter.8

commit v2 on v1

v2 whole, which is shorter than its diff:
```python
import functools

import jax
import jax.numpy as jnp
from jax import lax
from jax.experimental import pallas as pl
from jax.experimental.pallas import tpu as pltpu
from jax.sharding import Mesh, PartitionSpec as P

HEAD = 64
ROT = 16
STEP = 10

norm_eps = 1e-05
mask_fill = -1000000000.0
rope_base = 10000.0
beta_one = 0.9
beta_two = 0.95
adam_eps = 1e-08
rate_matrix = 0.01
rate_small = 0.1
decay_matrix = 0.1

LOW = jnp.bfloat16
FULL = jnp.float32

OUTER = ("y", "z")
GROUP = ("x", "core")
EVERY = OUTER + GROUP
RING = 4
MEMBERS = 8
OUTERS = 16


def product(left, right, dims):
    return lax.dot_general(left, right, (dims, ((), ())), preferred_element_type=FULL)


def normalize(values):
    center = values - jnp.mean(values, axis=-1, keepdims=True)
    spread = jnp.mean(center * center, axis=-1, keepdims=True)
    scaled = lax.rsqrt(spread + norm_eps)
    return (center * scaled, scaled)


def norm_back(grad_normed, normal, scaled, gain):
    grad_hat = grad_normed * gain
    return scaled * (
        grad_hat
        - jnp.mean(grad_hat, axis=-1, keepdims=True)
        - normal * jnp.mean(grad_hat * normal, axis=-1, keepdims=True)
    )


def rope_tables(rows, length, inner):
    half = ROT // 2
    lane = jnp.arange(inner) % HEAD
    position = (jnp.arange(rows) % length).astype(FULL)
    inverse = rope_base ** (-((lane % half).astype(FULL) * 2.0 / ROT))
    angle = position[:, None] * inverse[None, :]
    cosine = jnp.where(lane < ROT, jnp.cos(angle), 1.0)
    later = jnp.where(lane < half, -jnp.sin(angle), 0.0)
    earlier = jnp.where((lane >= half) & (lane < ROT), jnp.sin(angle), 0.0)
    return (cosine, later, earlier)


def rotate(values, tables, sign):
    cosine, later, earlier = tables
    half, lanes = (ROT // 2, values.shape[1])
    moved = pltpu.roll(values, lanes - half, 1) * later[...] + pltpu.roll(values, half, 1) * earlier[...]
    return values * cosine[...] + sign * moved


def pair_masks(length):
    rows = lax.broadcasted_iota(jnp.int32, (length, length), 0)
    columns = lax.broadcasted_iota(jnp.int32, (length, length), 1)
    lanes = lax.broadcasted_iota(jnp.int32, (length, 2 * HEAD), 1)
    return (rows >= columns, lanes < HEAD)


def soft(query, keyed, causal):
    scores = product(query, keyed, ((1,), (1,))) * HEAD**-0.5
    scores = jnp.where(causal, scores, mask_fill)
    weights = jnp.exp(scores - jnp.max(scores, axis=-1, keepdims=True))
    return weights / jnp.sum(weights, axis=-1, keepdims=True)


def out_columns(weights, inner, piece):
    start, step = (weights.shape[1] - inner, weights.shape[0] // OUTERS)
    rows = step // MEMBERS
    return jnp.concatenate(
        [weights[k * step + piece * rows : k * step + (piece + 1) * rows, start:] for k in range(OUTERS)], axis=0
    )


def attend_kernel(count, *refs):
    tokens, (weights, norm, bias, *tables) = (refs[:count], refs[count : count + 6])
    normed, turned, mixed, *branches = refs[count + 6 :]
    length, inner = (tokens[0].shape[0], bias.shape[1] // 3)
    causal, first = pair_masks(length)
    for block, part in enumerate(tokens):
        rows = slice(block * length, (block + 1) * length)
        normal, _ = normalize(part[...].astype(FULL))
        normed[rows] = (normal * norm[0:1] + norm[1:2]).astype(LOW)
    projected = product(normed[...], weights[:, : 3 * inner], ((1,), (0,))) + bias[...]
    for block in range(count):
        rows = slice(block * length, (block + 1) * length)
        query = rotate(projected[rows, :inner], tables, 1.0).astype(LOW)
        keyed = rotate(projected[rows, inner : 2 * inner], tables, 1.0).astype(LOW)
        valued = projected[rows, 2 * inner :].astype(LOW)
        turned[rows, :inner] = query
        turned[rows, inner : 2 * inner] = keyed
        turned[rows, 2 * inner :] = valued
        for column in range(0, inner, 2 * HEAD):
            at = slice(column, column + 2 * HEAD)
            outs = []
            for side in (first, ~first):
                prob = soft(jnp.where(side, query[:, at], 0), keyed[:, at], causal).astype(LOW)
                outs.append(product(prob, valued[:, at], ((1,), (0,))))
            mixed[rows, at] = jnp.where(first, outs[0], outs[1]).astype(LOW)
    half = length * count // 2
    for piece in range(MEMBERS):
        share = product(mixed[...], out_columns(weights, inner, piece), ((1,), (0,))).astype(LOW)
        for at, branch in enumerate(branches):
            branch[:, piece * inner : (piece + 1) * inner] = share[at * half : (at + 1) * half]


def attend(blocks, weights, norm, bias, tables):
    length, width = blocks[0].shape
    rows, inner = (length * len(blocks), bias.shape[1] // 3)
    shapes = ((rows, width), (rows, 3 * inner), (rows, inner), (rows // 2, width), (rows // 2, width))
    return pl.pallas_call(
        functools.partial(attend_kernel, len(blocks)),
        out_shape=[jax.ShapeDtypeStruct(shape, LOW) for shape in shapes],
        compiler_params=pltpu.CompilerParams(vmem_limit_bytes=28 << 20),
        cost_estimate=pl.CostEstimate(flops=10**9, bytes_accessed=rows * width, transcendentals=0),
        name="attend",
    )(*blocks, weights, norm, bias, *tables)


def attend_back_kernel(count, places, *refs):
    grads, tokens, refs = (refs[:count], refs[count : 2 * count], refs[2 * count :])
    weights, turned, sums_in, norm_in, *tables = refs[:7]
    back, sums, norm_sums, shares, back_mixed, normed_grad, low_grad, sent = refs[8:]
    length, inner = (grads[0].shape[0], turned.shape[1] // 3)
    total = 0.0
    for piece in range(MEMBERS):
        columns = slice(piece * inner, (piece + 1) * inner)
        rows = jnp.concatenate([grad[:, columns] for grad in grads], axis=0)
        total += product(rows, out_columns(weights, inner, piece), ((1,), (1,)))
    back_mixed[...] = total.astype(LOW)
    causal, first = pair_masks(length)
    bias_total = sums_in[...]
    for block in range(count):
        rows = slice(block * length, (block + 1) * length)
        parts = []
        for column in range(0, inner, 2 * HEAD):
            query, keyed, valued = (
                turned[rows, part * inner + column : part * inner + column + 2 * HEAD] for part in range(3)
            )
            grad_pair = back_mixed[rows, column : column + 2 * HEAD]
            back_query, back_key, back_value = ([], 0.0, 0.0)
            for side in (first, ~first):
                query_one = jnp.where(side, query, 0)
                grad_one = jnp.where(side, grad_pair, 0)
                prob = soft(query_one, keyed, causal)
                back_value += product(prob.astype(LOW), grad_one, ((0,), (0,)))
                grad_prob = product(grad_one, valued, ((1,), (1,)))
                delta = jnp.sum(prob * grad_prob, axis=-1, keepdims=True)
                grad_scores = (prob * (grad_prob - delta)).astype(LOW)
                back_query.append(product(grad_scores, keyed, ((1,), (0,))))
                back_key += product(grad_scores, query_one, ((0,), (0,)))
            back_query = jnp.where(first, back_query[0], back_query[1]) * HEAD**-0.5
            parts.append((back_query, back_key * HEAD**-0.5, back_value))
        back_query, back_key, back_value = (jnp.concatenate(side, axis=1) for side in zip(*parts))
        back[rows, :inner] = rotate(back_query, tables, -1.0).astype(LOW)
        back[rows, inner : 2 * inner] = rotate(back_key, tables, -1.0).astype(LOW)
        back[rows, 2 * inner :] = back_value.astype(LOW)
        bias_total += jnp.sum(back[rows].astype(FULL), axis=0, keepdims=True)
    sums[...] = bias_total
    normed_grad[...] = product(back[...], weights[:, : 3 * inner], ((1,), (1,)))
    scale_total, shift_total = (norm_in[0:8], norm_in[8:16])
    leaving = []
    for block in range(count):
        rows = slice(block * length, (block + 1) * length)
        low_grad[rows] = normed_grad[rows].astype(LOW)
        there = pl.ds(pl.multiple_of(places[block] * length, length), length)
        leaving.append(pltpu.make_async_copy(low_grad.at[rows], shares.at[there], sent.at[block]))
        leaving[-1].start()
    for block in range(count):
        rows = slice(block * length, (block + 1) * length)
        grad = normed_grad[rows]
        normal, _ = normalize(tokens[block][...].astype(FULL))
        scale_total += jnp.sum(grad * normal, axis=0, keepdims=True)
        shift_total += jnp.sum(grad, axis=0, keepdims=True)
    norm_sums[0:8] = scale_total
    norm_sums[8:16] = shift_total
    for copy in leaving:
        copy.wait()


def attend_back(places, grads, tokens, weights, turned, sums, norm_sums, shares, tables, micros):
    length, width = grads[0].shape
    count, (rows, columns) = (len(grads), turned.shape)
    made = (jax.ShapeDtypeStruct((rows, columns), LOW), sums, norm_sums, shares)
    operands = (places, *grads, *tokens, weights, turned, sums, norm_sums, *tables, shares)
    vmem, away = (pl.BlockSpec(memory_space=pltpu.VMEM), pl.BlockSpec(memory_space=pltpu.HBM))
    return pl.pallas_call(
        functools.partial(attend_back_kernel, count),
        in_specs=[pl.BlockSpec(memory_space=pltpu.SMEM)] + [vmem] * (len(operands) - 2) + [away],
        out_specs=[vmem] * 3 + [away],
        out_shape=[jax.ShapeDtypeStruct(m.shape, m.dtype) for m in made],
        scratch_shapes=[
            pltpu.VMEM((rows, columns // 3), LOW),
            pltpu.VMEM((rows, width), FULL),
            pltpu.VMEM((rows, width), LOW),
            pltpu.SemaphoreType.DMA((count,)),
        ],
        input_output_aliases={len(operands) - 1: 3},
        compiler_params=pltpu.CompilerParams(vmem_limit_bytes=28 << 20),
        cost_estimate=pl.CostEstimate(flops=micros * 10**9, bytes_accessed=rows * width, transcendentals=0),
        name="attend_back",
    )(*operands)


def residual_kernel(tokens, mine, arrived, twin, norm, residual, normed):
    total = tokens[...].astype(FULL) + mine[...].astype(FULL) + arrived[...].astype(FULL) + twin[...].astype(FULL)
    residual[...] = total
    normal, _ = normalize(total)
    normed[...] = (normal * norm[2:3] + norm[3:4]).astype(LOW)


def norm_back_kernel(given, row, low, values, base, *refs):
    grad = sum(g[...].astype(FULL) for g in refs[:given])
    norm, outs = (refs[given], refs[given + 1 :])
    normal, scaled = normalize(values[...].astype(FULL))
    total = base[...].astype(FULL) + norm_back(grad, normal, scaled, norm[row : row + 1])
    outs[0][...] = total
    if low:
        outs[1][...] = total.astype(LOW)

        @pl.when(pl.program_id(0) == 0)
        def _():
            outs[2][...] = jnp.zeros_like(outs[2])

        outs[2][0:8] += jnp.broadcast_to(jnp.sum(grad * normal, axis=0, keepdims=True), (8, grad.shape[1]))
        outs[2][8:16] += jnp.broadcast_to(jnp.sum(grad, axis=0, keepdims=True), (8, grad.shape[1]))


def by_rows(kernel, rows, operands, norm, shapes, name):
    block = rows // 4
    width = operands[0].shape[1]
    spot = pl.BlockSpec((block, width), lambda i: (i, 0))
    whole = [pl.BlockSpec(norm.shape, lambda i: (0, 0))] if norm is not None else []
    return pl.pallas_call(
        kernel,
        grid=(4,),
        in_specs=[spot] * len(operands) + whole,
        out_specs=[spot if shape[0] == rows else pl.BlockSpec(shape, lambda i: (0, 0)) for shape, _ in shapes],
        out_shape=[jax.ShapeDtypeStruct(shape, kind) for shape, kind in shapes],
        compiler_params=pltpu.CompilerParams(vmem_limit_bytes=16 << 20),
        cost_estimate=pl.CostEstimate(flops=10**8, bytes_accessed=10**6, transcendentals=0),
        name=name,
    )(*operands, *([norm] if whole else []))


def join_kernel(first, second, both):
    rows = first.shape[0]
    both[:rows] = first[...]
    both[rows:] = second[...]


def join_rows(first, second):
    rows, width = first.shape
    return pl.pallas_call(
        join_kernel,
        out_shape=jax.ShapeDtypeStruct((2 * rows, width), first.dtype),
        compiler_params=pltpu.CompilerParams(vmem_limit_bytes=8 << 20),
        cost_estimate=pl.CostEstimate(flops=1, bytes_accessed=1, transcendentals=0),
        name="join_rows",
    )(first, second)


def weight_grad_kernel(sizes, *refs):
    out, at, column = (refs[-1], 0, 0)
    for count in sizes:
        if count:
            lefts, rights = (refs[at : at + count[0]], refs[at + count[0] : at + sum(count)])
            total, rights = (0.0, list(rights))
            for left in lefts:
                right = [rights.pop(0)[...]]
                while sum(r.shape[0] for r in right) < left.shape[0]:
                    right.append(rights.pop(0)[...])
                total += product(left[...], jnp.concatenate(right, axis=0), ((0,), (0,)))
            at += sum(count)
        else:
            total = refs[at][...]
            if total.shape[0] == 8:
                total = jnp.concatenate([total, jnp.zeros((120, total.shape[1]), FULL)], axis=0).T
            at += 1
        out[:, column : column + total.shape[1]] = total.astype(LOW)
        column += total.shape[1]


def weight_grad(terms, block, limit):
    sizes, operands, specs, wide = ([], [], [], 0)
    for term in terms:
        if isinstance(term, tuple):
            lefts, rights = term
            height = lefts[0].shape[1]
            rows = min(block, height)
            columns = rights[0].shape[1]
            sizes.append((len(lefts), len(rights)))
            operands += [*lefts, *rights]
            specs += [pl.BlockSpec((left.shape[0], rows), lambda i: (0, i)) for left in lefts]
            specs += [pl.BlockSpec(right.shape, lambda i: (0, 0)) for right in rights]
        elif term.shape[0] == 8:
            columns = 128
            sizes.append(())
            operands.append(term)
            specs.append(pl.BlockSpec((8, rows), lambda i: (0, i)))
        else:
            columns = term.shape[1]
            sizes.append(())
            operands.append(term)
            specs.append(pl.BlockSpec((rows, columns), lambda i: (i, 0)))
        wide += columns
    return pl.pallas_call(
        functools.partial(weight_grad_kernel, tuple(sizes)),
        grid=(height // rows,),
        in_specs=specs,
        out_specs=pl.BlockSpec((rows, wide), lambda i: (i, 0)),
        out_shape=jax.ShapeDtypeStruct((height, wide), LOW),
        compiler_params=pltpu.CompilerParams(vmem_limit_bytes=limit << 20),
        cost_estimate=pl.CostEstimate(flops=height * wide, bytes_accessed=height * wide, transcendentals=0),
        name="weight_grad",
    )(*operands)


def adamw(weight, grad, first, second, rate, decay):
    first_new = beta_one * first + (1.0 - beta_one) * grad
    second_new = beta_two * second + (1.0 - beta_two) * grad * grad
    corr_one = 1.0 - beta_one**STEP
    corr_two = 1.0 - beta_two**STEP
    update = first_new / corr_one / (jnp.sqrt(second_new / corr_two) + adam_eps)
    return (weight - rate * (update + decay * weight), first_new, second_new)


def adamw_kernel(skip, pieces, weight, first, second, *outs):
    rows, wide = (weight.shape[0], weight.shape[1] // (pieces.shape[0] // 2))
    half = wide // 2
    across = -(-half // 128) * 128
    lanes = lax.broadcasted_iota(jnp.int32, (rows, wide), 1)
    blank = jnp.zeros((rows, wide - across), FULL)

    def turned(member, start, target):
        base = start // 128 * 128
        values = pieces[member, :, base : base + across].astype(FULL)
        move = (target - (start - base)) % across
        return pltpu.roll(values, move, 1) if move else values

    for part in range(3):

        @pl.when(pl.program_id(0) == part)
        def _():
            start = skip + part * half
            for pair in range(pieces.shape[0] // 2):
                left = jnp.concatenate([turned(2 * pair, start, 0), blank], axis=1)
                right = jnp.concatenate([blank, turned(2 * pair + 1, start, across - half)], axis=1)
                grad = jnp.where(lanes < half, left, right)
                at = (slice(None), slice(pair * wide, (pair + 1) * wide))
                made = adamw(weight[at], grad, first[at], second[at], rate_matrix, decay_matrix)
                for out, value in zip(outs, made):
                    out[at] = value


def adamw_mlp(pieces, skip, weight, first, second):
    rows, width = weight.shape
    spot = pl.BlockSpec((rows, width // 3), lambda part: (0, part))
    return pl.pallas_call(
        functools.partial(adamw_kernel, skip),
        grid=(3,),
        in_specs=[pl.BlockSpec(pieces.shape, lambda part: (0, 0, 0))] + [spot] * 3,
        out_specs=[spot] * 3,
        out_shape=[jax.ShapeDtypeStruct(weight.shape, FULL)] * 3,
        compiler_params=pltpu.CompilerParams(vmem_limit_bytes=24 << 20),
        cost_estimate=pl.CostEstimate(flops=10**8, bytes_accessed=7 * 4 * weight.size, transcendentals=0),
        name="adamw",
    )(pieces, weight, first, second)


def shift(values, axis, hop):
    return lax.ppermute(values, axis, [(i, (i + hop) % RING) for i in range(RING)])


def sibling(values):
    return lax.ppermute(values, "core", [(0, 1), (1, 0)])


def add(*values):
    return sum(v.astype(FULL) for v in values)


def hold(values, *others):
    return lax.optimization_barrier((values, others))[0]


def blocks_at(rows, places, length, column):
    width = rows.shape[1] // 2
    return [lax.dynamic_slice(rows, (place * length, column), (length, width)) for place in places]


def onward(values, back=False):
    moves = []
    for chip in range(RING):
        for core, hop in ((0, 1), (1, -1)):
            moves.append((2 * chip + core, 2 * ((chip + (-hop if back else hop)) % RING) + core))
    return lax.ppermute(values, GROUP, moves)


def group_places():
    chip, core = (lax.axis_index(axis) for axis in GROUP)
    one, two, far = ((chip + 3 + 2 * core) % RING, (chip + 1 + 2 * core) % RING, (chip + 2) % RING)
    other = 1 - core
    parts = (
        [2 * chip + core, 2 * chip + other],
        [2 * one + core, 2 * one + other, 2 * two + other, 2 * two + core],
        [2 * far + core, 2 * far + other],
    )
    return [jnp.stack(part).astype(jnp.int32) for part in parts]


def gather_group(values, work):
    rows = values.shape[0]
    own = join_rows(values, sibling(values))
    one = onward(own)
    parts = [[own[:rows], own[rows:]]]
    done = [work(0, parts[0])]
    one = hold(one, done[0][-1])
    far = onward(one[:rows])
    two = sibling(one)
    parts.append([one[:rows], one[rows:], two[:rows], two[rows:]])
    done.append(work(1, parts[1]))
    far = hold(far, done[1][-1])
    parts.append([far, sibling(far)])
    done.append(work(2, parts[2]))
    return (parts, done)


class Scatter:
    def far(self, blocks):
        self.sum = add(blocks[0], sibling(blocks[1])).astype(LOW)
        return self.sum

    def first(self):
        self.arrived = onward(self.sum, back=True)
        return self.arrived

    def near(self, blocks):
        self.both = add(blocks[0], sibling(blocks[1]))
        self.rows = self.both.shape[0] // 2
        return self.both

    def merge(self):
        rows = self.rows
        self.sum = jnp.concatenate([add(self.both[:rows], self.arrived), self.both[rows:]], axis=0).astype(LOW)
        return self.sum

    def second(self):
        self.arrived = onward(self.sum, back=True)
        return self.arrived

    def own(self, whole):
        rows = self.rows
        twin = sibling(add(whole[rows:], self.arrived[rows:]).astype(LOW))
        return (whole, self.arrived, twin)


def gather_outer(values):
    rows, columns = values.shape
    half = rows // 2
    place = {axis: lax.axis_index(axis) for axis in OUTER}

    def ring(block, axis, straight=False):
        before = shift(block, axis, 1)
        after = shift(block, axis, -1)
        if straight:
            return zip((block, before, after, shift(block, axis, 2)), [(place[axis] + j) % RING for j in (0, 3, 1, 2)], (0,) * 4)
        quarter = block.shape[0] // 2
        far = (shift(before[:quarter], axis, 1), shift(after[quarter:], axis, -1))
        spots = [(place[axis] + j) % RING for j in (0, 3, 1, 2, 2)]
        return zip((block, before, after, *far), spots, (0, 0, 0, 0, quarter))

    lines = []
    for axis, block in (("z", values[:half]), ("y", values[half:])):
        line = jnp.zeros((RING, half, columns), values.dtype)
        for piece, spot, start in ring(block, axis, True):
            line = lax.dynamic_update_slice(line, piece[None], (spot, start, 0))
        lines.append(line)
    whole = jnp.zeros((RING, RING, 2, half, columns), values.dtype)
    rings = [list(ring(line, axis)) for line, axis in zip(lines, ("y", "z"))]
    for piece, spot, start in rings[0]:
        whole = lax.dynamic_update_slice(whole, piece[None, :, None], (spot, start, 0, 0, 0))
    for piece, spot, start in rings[1]:
        whole = lax.dynamic_update_slice(whole, piece[:, None, None], (start, spot, 1, 0, 0))
    return whole.reshape(OUTERS * rows, columns)


def far_step(far, axis):
    half = far.shape[0] // 2
    return (shift(far[:half], axis, 1), shift(far[half:], axis, -1))


def near_shares(next_part, last_part, arrived):
    up, down = arrived
    half = up.shape[0]
    after = lax.dynamic_update_slice_in_dim(next_part, add(next_part[:half], up).astype(LOW), 0, 0)
    before = lax.dynamic_update_slice_in_dim(last_part, add(last_part[half:], down).astype(LOW), half, 0)
    return (after, before)


def near_step(shares, axis):
    return (shift(shares[0], axis, 1), shift(shares[1], axis, -1))


def reduce_ring(parts, axis):
    return add(parts[0], *(shift(parts[j], axis, j) for j in (1, 3, 2)))


def ring_order(values, axis, dim):
    place = lax.axis_index(axis)
    return [lax.dynamic_index_in_dim(values, (place + j) % RING, dim, keepdims=False) for j in range(RING)]


def block_moves(back):
    moves = []
    for outer in range(OUTERS):
        for member in range(MEMBERS):
            owner = member * OUTERS + outer
            here = outer * MEMBERS + member
            moves.append((here, owner) if back else (owner, here))
    return moves


def spread_columns(block, parts):
    rows = block.shape[0]
    return block.reshape(rows, parts, MEMBERS, -1).transpose(2, 0, 1, 3).reshape(MEMBERS, rows, -1)


def join_columns(pieces, parts):
    members, rows, width = pieces.shape
    turned = pieces.reshape(members, rows, parts, width // parts).transpose(1, 2, 0, 3)
    return turned.reshape(rows, members * width)


def local(
    tokens,
    cotangent,
    attn_weight,
    mlp_weight,
    small_weight,
    attn_first,
    attn_second,
    mlp_first,
    mlp_second,
    small_first,
    small_second,
):
    length, width = tokens.shape
    own_rows = attn_weight.shape[0]
    slab = own_rows * MEMBERS
    hidden = mlp_weight.shape[1] // 3 // MEMBERS
    inner = width // MEMBERS
    heads = inner // HEAD
    member = lax.axis_index(GROUP)

    rows_all = lax.all_gather(jnp.concatenate([tokens, cotangent], axis=1), GROUP, axis=0, tiled=True)

    attn_low = attn_weight.astype(LOW)
    small_low = jnp.pad(small_weight.astype(LOW).T, ((0, 0), (0, 121)))
    columns = 3 * inner + 128
    sent = jnp.concatenate(
        [
            spread_columns(attn_low[:, : 3 * width], 3),
            jnp.broadcast_to(small_low, (MEMBERS, own_rows, 128)),
            spread_columns(mlp_weight.astype(LOW), 3),
        ],
        axis=2,
    )
    slabs = lax.all_to_all(sent, GROUP, 0, 0, tiled=True).reshape(slab, columns + 3 * hidden)
    out_block = lax.ppermute(attn_low[:, 3 * width :], EVERY, block_moves(False))
    out_block = out_block.reshape(own_rows, MEMBERS, inner).transpose(1, 0, 2).reshape(slab, inner)
    mlp_part = lax.all_gather(slabs[:, columns:], OUTER, axis=0, tiled=True)
    places = group_places()
    tokens_all = [blocks_at(rows_all, part, length, 0) for part in places]
    attn_part = gather_outer(jnp.concatenate([slabs[:, :columns], out_block], axis=1))
    params = attn_part[:, 3 * inner : 3 * inner + 7].T.astype(FULL)
    bias = lax.dynamic_slice_in_dim(params[4:7], member * inner, inner, axis=1).reshape(1, -1)
    weight_wide = mlp_part[:, : 2 * hidden]
    weight_down = mlp_part[:, 2 * hidden :]

    tables = rope_tables(length, length, inner)
    cotangent_all = [jnp.concatenate(blocks_at(rows_all, part, length, width), axis=0) for part in places]

    def forward(blocks):
        return attend(blocks, attn_part, params[:2], bias, tables)

    ring = Scatter()
    kept = {2: forward(tokens_all[2])}
    ring.far(kept[2][3:])
    near_in = hold(tokens_all[1], ring.sum)
    ring.first()
    kept[1] = forward(near_in)
    ring.near(hold(kept[1][3:], ring.arrived))
    own_in, cotangent_all = hold((tokens_all[0], cotangent_all), ring.merge())
    own_in = hold(own_in, cotangent_all)
    ring.second()
    kept[0] = forward(own_in)
    ring.arrived = hold(ring.arrived, kept[0][3:])
    residual, normed_two = by_rows(
        residual_kernel,
        length,
        (tokens, kept[0][3], ring.arrived, sibling(add(kept[0][4], ring.arrived[length:]).astype(LOW))),
        params,
        (((length, width), FULL), ((length, width), LOW)),
        "residual",
    )
    normed_low, turned, mixed_low = ([kept[p][i] for p in range(3)] for i in range(3))

    def feed(part, blocks):
        rows = jnp.concatenate(blocks, axis=0)
        both = product(rows, weight_wide, ((1,), (0,)))
        gate, upward = (both[:, :hidden], both[:, hidden:])
        sigma = jax.nn.sigmoid(gate)
        active = gate * sigma
        hidden_low = (active * upward).astype(LOW)
        back_hidden = product(cotangent_all[part], weight_down, ((1,), (0,)))
        back_gate = (back_hidden * upward * sigma * (1.0 + gate * (1.0 - sigma))).astype(LOW)
        back_wide = jnp.concatenate([back_gate, (back_hidden * active).astype(LOW)], axis=1)
        share = product(back_wide, weight_wide, ((1,), (1,))).astype(LOW)
        return (rows, hidden_low, back_wide, share)

    def halves_of(rows):
        half = rows.shape[0] // 2
        return (rows[:half], rows[half:])

    def out_share(part):
        return product(hidden_low[part], weight_down, ((1,), (1,))).astype(LOW)

    _, done = gather_group(normed_two, feed)
    normed_two, hidden_low, back_wide, shares = (list(made) for made in zip(*done))
    ring = Scatter()
    ring.near(halves_of(shares[1]))
    ring.far(halves_of(shares[2]))
    hidden_low = hold(hidden_low, ring.sum)
    ring.first()
    out_shares = [out_share(part) for part in range(3)]
    ring.arrived = hold(ring.arrived, out_shares)
    ring.merge()
    back_wide = hold(back_wide, ring.sum)
    ring.second()
    mlp_grad = weight_grad([(normed_two, back_wide), (cotangent_all, hidden_low)], 512, 36)
    ring.arrived = hold(ring.arrived, mlp_grad)
    back_residual, back_low, norm_two_grads = by_rows(
        functools.partial(norm_back_kernel, 3, 2, True),
        length,
        (residual, cotangent, *ring.own(shares[0])),
        params,
        (((length, width), FULL), ((length, width), LOW), ((16, width), FULL)),
        "norm_back",
    )
    mlp_grad = lax.psum_scatter(mlp_grad, OUTER, scatter_dimension=0, tiled=True)

    back_sums = [jnp.zeros((8, 3 * inner), FULL), jnp.zeros((16, width), FULL), jnp.zeros((MEMBERS * length, width), LOW)]
    ring = Scatter()
    taken, out_grads = ([], [])

    def out_grad():
        grad = weight_grad([(mixed_low, taken)], inner, 16)
        grad = grad.reshape(OUTERS, own_rows, MEMBERS, inner).transpose(0, 2, 1, 3)
        return grad.reshape(width, inner)

    def backward(part, blocks):
        if part == 1:
            ring.far(hold(halves_of(out_shares[2]), blocks[0]))
            blocks = hold(blocks, ring.sum)
            ring.first()
        elif part == 2:
            ring.near(halves_of(out_shares[1]))
            blocks = hold(blocks, ring.merge())
            ring.second()
        taken.extend(blocks)
        if part == 2:
            out_grads[:] = [out_grad()]
            blocks = hold(blocks, out_grads)
        made = attend_back(
            places[part], blocks, tokens_all[part], attn_part, turned[part], *back_sums, tables, (20, 40, 20)[part]
        )
        back_sums[:] = made[1:]
        return made[:2]

    _, done = gather_group(back_low, backward)
    back_proj = [made[0] for made in done]

    bias_rows = jnp.pad(
        back_sums[0][0].reshape(3, OUTERS, own_rows), ((0, 0), (0, 0), (0, slab - own_rows))
    ).reshape(3, width)
    small_rows = jnp.concatenate(
        [
            back_sums[1][:1],
            back_sums[1][8:9],
            norm_two_grads[:1],
            norm_two_grads[8:9],
            bias_rows,
            jnp.zeros((1, width), FULL),
        ],
        axis=0,
    )
    back_proj = hold(back_proj, ring.arrived)
    attn_grad = weight_grad([(normed_low, back_proj), small_rows, out_grads[0]], 512, 60)
    output = add(residual, *(rows[:length] for rows in ring.own(hold(out_shares[0], attn_grad))))
    blocks = attn_grad.reshape(RING, RING, 2, slab // 2, -1)
    parts = [ring_order(blocks[:, :, half], axis, half) for half, axis in enumerate(OUTER)]
    arrived = [far_step(part[2], axis) for part, axis in zip(parts, OUTER)]
    shares = [near_shares(part[1], part[3], halves) for part, halves in zip(parts, arrived)]
    totals = [
        add(part[0], *near_step(share, axis)).astype(LOW) for part, share, axis in zip(parts, shares, OUTER)
    ]
    back_normed_one = lax.psum_scatter(hold(back_sums[2], shares), GROUP, scatter_dimension=0, tiled=True)
    totals = hold(totals, mlp_grad, output)
    totals = [reduce_ring(ring_order(total, axis, 0), axis).astype(LOW) for total, axis in zip(totals, OUTER[::-1])]
    attn_grad = hold(jnp.concatenate(totals, axis=0), back_normed_one)
    (grad_tokens,) = by_rows(
        functools.partial(norm_back_kernel, 1, 0, False),
        length,
        (tokens, back_residual, back_normed_one),
        params,
        (((length, width), FULL),),
        "norm_back",
    )
    out_grad = (
        attn_grad[:, 3 * inner + 128 :]
        .reshape(MEMBERS, own_rows, inner)
        .transpose(1, 0, 2)
        .reshape(own_rows, width)
    )
    bias_grad = attn_grad[:own_rows, 3 * inner : 3 * inner + 128]
    block = lax.ppermute(
        jnp.concatenate([out_grad, bias_grad], axis=1), EVERY, block_moves(True)
    ).astype(FULL)
    blank = jnp.zeros((slab, -(columns + 3 * hidden) % 128), LOW)
    pieces = jnp.concatenate([attn_grad[:, :columns], mlp_grad, blank], axis=1).reshape(MEMBERS, own_rows, -1)
    all_pieces = lax.all_to_all(pieces, GROUP, 0, 0, tiled=True)
    pieces = all_pieces[:, :, :columns].astype(FULL)
    attn_grad = jnp.concatenate(
        [join_columns(pieces[:, :, : 3 * inner], 3), block[:, :width]], axis=1
    )
    norm_grads = jnp.sum(pieces[:, :, 3 * inner : 3 * inner + 4], axis=0)
    small_grad = jnp.concatenate([norm_grads, block[:, width + 4 : width + 7]], axis=1).T

    attn_new, attn_first_new, attn_second_new = adamw(
        attn_weight, attn_grad, attn_first, attn_second, rate_matrix, decay_matrix
    )
    mlp_new, mlp_first_new, mlp_second_new = adamw_mlp(all_pieces, columns, mlp_weight, mlp_first, mlp_second)
    small_new, small_first_new, small_second_new = adamw(
        small_weight, small_grad, small_first, small_second, rate_small, 0.0
    )
    return (
        output.astype(LOW),
        grad_tokens,
        attn_new,
        attn_first_new,
        attn_second_new,
        mlp_new,
        mlp_first_new,
        mlp_second_new,
        small_new,
        small_first_new,
        small_second_new,
    )


def solution(mesh):
    grid = Mesh(mesh.devices.reshape(4, 4, 4, 2), EVERY)
    rows, columns = (P(EVERY, None), P(None, EVERY))
    return jax.shard_map(
        local,
        mesh=grid,
        in_specs=(rows,) * 4 + (columns,) + (rows,) * 4 + (columns,) * 2,
        out_specs=(rows,) * 8 + (columns,) * 3,
        check_vma=False,
    )
```

time: 570 us -> 384 us (0.67)
  waiting for transfers between devices: 239 us -> 94.8 us
  Pallas kernels: 0 us -> 81.5 us
  local copies, waits for them, and re-layouts: 107 us -> 47 us
  matrix products: 73.9 us -> 29.9 us
  other arithmetic: 50.2 us -> 21.9 us
  starting transfers between devices: 74.6 us -> 85.4 us
    pallas_call x0 -> x15, Pallas kernels: none -> 81.5 us  [the longest x3 27.8 us: attend_back(): pl.pallas_call(functools.partial(attend_back_kernel, count), in_specs=[pl...]
    reduce_scatter x1, waiting for transfers between devices: 71.8 us -> 0.02 us  [local(): lax.psum_scatter(mlp_grad, OUTER, scatter_dimension=0, tiled=True)]
    reduce_scatter x1, waiting for transfers between devices: 48.9 us -> 0.02 us  [local(): lax.psum_scatter(hold(back_sums[2], shares), GROUP, scatter_dimension=0,...]
    ppermute x32 -> x38, waiting for transfers between devices: 93.9 us -> 47 us  [the longest x28 35.2 us: shift(): lax.ppermute(values, axis, [(i, (i + hop) % RING) for i in range(RING)])]
    unnamed x176 -> x171, local copies, waits for them, and re-layouts: 57.2 us -> 22.5 us
    dot_general x12, matrix products: 64.1 us -> 29.9 us  [product(): lax.dot_general(left, right, (dims, ((), ())), preferred_element_type=FULL)]
    ppermute x32 -> x38, starting transfers between devices: 38.3 us -> 60.9 us  [the longest x28 42.5 us: shift(): lax.ppermute(values, axis, [(i, (i + hop) % RING) for i in range(RING)])]
    ppermute x1, waiting for transfers between devices: 0.27 us -> 13.3 us  [local(): lax.ppermute(jnp.concatenate([out_grad, bias_grad], axis=1), EVERY, block...]
  transfers between devices with their start and end apart: 62 -> 61, of which waited for: 30 -> 31; matrix products, arithmetic and copies ran while one was open for 28% -> 18% of each run, Pallas kernels for 0% -> 21%
where the time goes in v2:
time: 384 us; the launch traced here: 377 us
  waiting for transfers between devices  94.8 us (25%)
  starting transfers between devices  85.4 us (22%)
  Pallas kernels  81.5 us (21%)
  local copies, waits for them, and re-layouts  47 us (12%)
  matrix products  29.9 us (8%)
  other arithmetic  21.9 us (6%)
  between operations  16.1 us (4%)
    ppermute x28, starting transfers between devices, shift(): lax.ppermute(values, axis, [(i, (i + hop) % RING) for i in range(RING)])  42.5 us
    ppermute x28, waiting for transfers between devices, shift(): lax.ppermute(values, axis, [(i, (i + hop) % RING) for i in range(RING)])  35.2 us
    dot_general x12, matrix products, product(): lax.dot_general(left, right, (dims, ((), ())), preferred_element_type=FULL)  29.9 us
    pallas_call x3, Pallas kernels, attend_back(): pl.pallas_call(functools.partial(attend_back_kernel, count), in_specs=[pl...  27.8 us
    pallas_call x3, Pallas kernels, weight_grad(): pl.pallas_call(functools.partial(weight_grad_kernel, tuple(sizes)), grid=...  22.9 us
    unnamed x171, local copies, waits for them, and re-layouts  22.5 us
    ppermute x10, starting transfers between devices, onward(): return lax.ppermute(values, GROUP, moves)  18.4 us
    pallas_call x3, Pallas kernels, attend(): pl.pallas_call(functools.partial(attend_kernel, len(blocks)), out_shape=[...  18.2 us
  transfers between devices with their start and end apart: 61, of which 31 were waited for; matrix products, arithmetic and copies ran while one was open for 18% of the time, Pallas kernels for 21%

profile of v2, /device:TPU:18, one launch (start us, length us, event | category | flops | bytes accessed | tf_op | source)
XLA Modules:
  0.0 376.6 jit_solution(3701863269432204434)
XLA Ops:
  13.4 4.8 %all-to-all-start = ((bf16[8,16,3008]{2,1,0:T(8,128)(2,1)}), bf16[8,16,3008]{2,1,0:T(8,128)(2,1)S(1)}, u32[]{:S(2)}, u32[]{:S(2)}) async-start(bf16[8,16,3008]{2,1,0:T(8,128)(2,1)} %pad_maximum_fusion.8), calls=%async_computation | async-start | bytes 1572864 | tf_op jit(solution)/shard_map/all_to_all | solution.py:590
  18.2 6.5 %collective-permute-start = (bf16[16,2048]{1,0:T(8,128)(2,1)S(1)}, bf16[16,2048]{1,0:T(8,128)(2,1)S(1)}, u32[]{:S(2)}, u32[]{:S(2)}) collective-permute-start(bf16[16,2048]{1,0:T(8,128)(2,1)S(1)} %slice.325), channel_id=1, source_target_pairs={{0,0},{16,1},{32,2},{48,3},{64,4},{80,5},{96,6},{112,7},{1,8},{17,... | collective-permute-start | bytes 196616 | tf_op jit(solution)/shard_map/ppermute | solution.py:591
  24.7 9.3 %all-to-all-done = bf16[8,16,3008]{2,1,0:T(8,128)(2,1)S(1)} async-done(((bf16[8,16,3008]{2,1,0:T(8,128)(2,1)}), bf16[8,16,3008]{2,1,0:T(8,128)(2,1)S(1)}, u32[]{:S(2)}, u32[]{:S(2)}) %all-to-all-start) | async-done | bytes 770080 | tf_op jit(solution)/shard_map/all_to_all | solution.py:590
  57.3 8.0 %collective-permute-done.4 = bf16[4,64,1152]{2,1,0:T(8,128)(2,1)S(1)} collective-permute-done((bf16[4,64,1152]{2,1,0:T(8,128)(2,1)S(1)}, bf16[4,64,1152]{2,1,0:T(8,128)(2,1)S(1)}, u32[]{:S(2)}, u32[]{:S(2)}) %collective-permute-start.4) | collective-permute-done | bytes 589856 | tf_op jit(solution)/shard_map/ppermute | solution.py:393
  70.3 3.7 collective-permute-start.14
  82.5 4.3 %constant_dynamic-slice_fusion.1 = (bf16[128,2048]{1,0:T(8,128)(2,1)S(1)}, bf16[128,2048]{1,0:T(8,128)(2,1)S(1)}, bf16[128,2048]{1,0:T(8,128)(2,1)S(1)}, bf16[12...) fusion(bf16[1024,4096]{1,0:T(8,128)(2,1)} %all-gather.3.cloned., ...), kind=kLoop, calls=%fused_computation.160 | loop fusion | bytes 16777248 | tf_op jit(solution)/shard_map/dynamic_slice | solution.py:410
  87.0 3.9 %copy-done.1 = bf16[4,4,2,64,1152]{4,3,2,1,0:T(8,128)(2,1)S(1)} copy-done((bf16[4,4,2,64,1152]{4,3,2,1,0:T(8,128)(2,1)S(1)}, bf16[4,4,2,64,1152]{4,3,2,1,0:T(8,128)(2,1)}, u32[]{:S(2)}) %copy-start.1) | copy-done | bytes 4718616
  90.8 4.6 %attend.3 = (bf16[256,2048]{1,0:T(8,128)(2,1)S(1)}, bf16[256,768]{1,0:T(8,128)(2,1)S(1)}, bf16[256,256]{1,0:T(8,128)(2,1)S(1)}, bf16[128,2048]{1,0:T(8,128)(2,1)S(1)}, bf16[128,2048]{1,0:T(8,128)(2,1)S(1)}) custom-call(bf16[128,2048]{1,0:T(8,128)(2,1)S(1)} %get-tuple-element.191.refs_0_.refs_2_, bf16[128,2048]{1,0:T(8,128)(2,1)S(1)} %get-tuple-element.190.refs_1_.refs_3_, ...), custom_call_target="tpu_custom_call" | custom-call | flops 1000000000 | bytes 524288 | tf_op jit(solution)/shard_map/attend/pallas_call | solution.py:132
  98.7 9.0 %attend.4 = (bf16[512,2048]{1,0:T(8,128)(2,1)S(1)}, bf16[512,768]{1,0:T(8,128)(2,1)S(1)}, bf16[512,256]{1,0:T(8,128)(2,1)S(1)}, bf16[256,2048]{1,0:T(8,128)(2,1)S(1)}, bf16[256,2048]{1,0:T(8,128)(2,1)S(1)}) custom-call(bf16[128,2048]{1,0:T(8,128)(2,1)S(1)} %get-tuple-element.92.refs_0_.refs_4_, bf16[128,2048]{1,0:T(8,128)(2,1)S(1)} %get-tuple-element.93.refs_1_.refs_5_, ...), custom_call_target="tpu_custom_call" | custom-call | flops 1000000000 | bytes 1048576 | tf_op jit(solution)/shard_map/attend/pallas_call | solution.py:132
  115.6 4.6 %attend.5 = (bf16[256,2048]{1,0:T(8,128)(2,1)S(1)}, bf16[256,768]{1,0:T(8,128)(2,1)S(1)}, bf16[256,256]{1,0:T(8,128)(2,1)S(1)}, bf16[128,2048]{1,0:T(8,128)(2,1)S(1)}, bf16[128,2048]{1,0:T(8,128)(2,1)S(1)}) custom-call(bf16[128,2048]{1,0:T(8,128)(2,1)S(1)} %get-tuple-element.105.refs_0_.refs_2_, bf16[128,2048]{1,0:T(8,128)(2,1)S(1)} %get-tuple-element.106.refs_1_.refs_3_, ...), custom_call_target="tpu_custom_call" | custom-call | flops 1000000000 | bytes 524288 | tf_op jit(solution)/shard_map/attend/pallas_call | solution.py:132
  120.3 5.9 %collective-permute-done.18.arrived = bf16[256,2048]{1,0:T(8,128)(2,1)S(1)} collective-permute-done((bf16[256,2048]{1,0:T(8,128)(2,1)S(1)}, bf16[256,2048]{1,0:T(8,128)(2,1)S(1)}, u32[]{:S(2)}, u32[]{:S(2)}) %collective-permute-start.18) | collective-permute-done | bytes 1048608 | tf_op jit(solution)/shard_map/ppermute | solution.py:418
  133.9 10.9 %all-gather.5.cloned.1.call-done = bf16[2048,2112]{1,0:T(8,128)(2,1)} async-done(((bf16[128,2112]{1,0:T(8,128)(2,1)}), bf16[2048,2112]{1,0:T(8,128)(2,1)}) %all-gather.5.cloned.1.call-update) | async-done | bytes 8650768 | tf_op jit(solution)/shard_map/all_gather | solution.py:593
  144.8 4.9 %fusion.7 = f32[256,1408]{1,0:T(8,128)S(1)} fusion(bf16[256,2048]{1,0:T(8,128)(2,1)} %join_rows.2.refs_0_, bf16[2048,2112]{1,0:T(8,128)(2,1)} %all-gather.5.cloned.1.call-done), kind=kOutput, calls=%fused_computation.13 | convolution fusion | flops 1476395008 | bytes 8257536 | tf_op jit(solution)/shard_map/dot_general | solution.py:36
  190.1 13.3 %weight_grad.3 = bf16[2048,2112]{1,0:T(8,128)(2,1)} custom-call(bf16[256,2048]{1,0:T(8,128)(2,1)} %join_rows.2.refs_0_, bf16[512,2048]{1,0:T(8,128)(2,1)S(1)} %constant_dynamic-update-slice_fusion.refs_1_, bf16[256,2048]{1,0:T(8,128)(2,1)S(1)} %constant_dynamic-update-slice_fusion.2.refs_2_, bf16[256,1408]{1,0:T(8,128)(2,1)S(1)} %pad_maximum_fusion.9.refs_3_, ...), custom_call_target="tpu_custom_call" | custom-call | flops 4325376 | bytes 4325376 | tf_op jit(solution)/shard_map/weight_grad/pallas_call | solution.py:328
  208.6 3.9 %norm_back.2 = (f32[128,2048]{1,0:T(8,128)S(1)}, bf16[128,2048]{1,0:T(8,128)(2,1)}, f32[16,2048]{1,0:T(8,128)S(1)}) custom-call(f32[128,2048]{1,0:T(8,128)S(1)} %get-tuple-element.110.values, bf16[128,2048]{1,0:T(8,128)(2,1)S(1)} %copy-done.27, bf16[256,2048]{1,0:T(8,128)(2,1)S(1)} %copy-done.9, bf16[256,2048]{1,0:T(8,128)(2,1)} %collective-permute-done.28.refs_1_, ...), custom_call_target="tpu_custom_call" | custom-call | flops 100000000 | bytes 1000000 | tf_op jit(solution)/shard_map/norm_back/pallas_call | solution.py:255
  220.2 7.1 %attend_back.3 = (bf16[256,768]{1,0:T(8,128)(2,1)S(1)}, f32[8,768]{1,0:T(8,128)S(1)}, f32[16,2048]{1,0:T(8,128)S(1)}, bf16[1024,2048]{1,0:T(8,128)(2,1)S(1)}) custom-call(s32[2]{0:T(128)S(1)} %get-tuple-element.252.places, bf16[128,2048]{1,0:T(8,128)(2,1)S(1)} %get-tuple-element.234.refs_0_.refs_3_, ...), custom_call_target="tpu_custom_call", output_to_operand_aliasing={{3}: (12, {})} | custom-call | flops 20000000000 | bytes 524288 | tf_op jit(solution)/shard_map/attend_back/pallas_call | solution.py:208
  227.3 5.6 %collective-permute-done.31 = bf16[256,2048]{1,0:T(8,128)(2,1)S(1)} collective-permute-done((bf16[256,2048]{1,0:T(8,128)(2,1)S(1)}, bf16[256,2048]{1,0:T(8,128)(2,1)S(1)}, u32[]{:S(2)}, u32[]{:S(2)}) %collective-permute-start.31) | collective-permute-done | bytes 1048608 | tf_op jit(solution)/shard_map/ppermute | solution.py:418
  240.1 13.5 %attend_back.4 = (bf16[512,768]{1,0:T(8,128)(2,1)S(1)}, f32[8,768]{1,0:T(8,128)S(1)}, f32[16,2048]{1,0:T(8,128)S(1)}, bf16[1024,2048]{1,0:T(8,128)(2,1)S(1)}) custom-call(s32[4]{0:T(128)S(1)} %pad_add_fusion.1.places, bf16[128,2048]{1,0:T(8,128)(2,1)S(1)} %get-tuple-element.132.refs_0_.refs_5_, ...), custom_call_target="tpu_custom_call", output_to_operand_aliasing={{3}: (16, {})} | custom-call | flops 40000000000 | bytes 1048576 | tf_op jit(solution)/shard_map/attend_back/pallas_call | solution.py:208
  260.7 7.1 %attend_back.5 = (bf16[256,768]{1,0:T(8,128)(2,1)S(1)}, f32[8,768]{1,0:T(8,128)S(1)}, f32[16,2048]{1,0:T(8,128)S(1)}, bf16[1024,2048]{1,0:T(8,128)(2,1)S(1)}) custom-call(s32[2]{0:T(128)S(1)} %get-tuple-element.253.places, bf16[128,2048]{1,0:T(8,128)(2,1)S(1)} %collective-permute-done.34.refs_9_.refs_0_, ...), custom_call_target="tpu_custom_call", output_to_operand_aliasing={{3}: (12, {})} | custom-call | flops 20000000000 | bytes 524288 | tf_op jit(solution)/shard_map/attend_back/pallas_call | solution.py:208
  272.1 8.3 %weight_grad.5 = bf16[2048,1152]{1,0:T(8,128)(2,1)} custom-call(bf16[256,2048]{1,0:T(8,128)(2,1)} %copy-done.37, bf16[512,2048]{1,0:T(8,128)(2,1)} %copy-done.26, bf16[256,2048]{1,0:T(8,128)(2,1)} %copy-done.36, bf16[256,768]{1,0:T(8,128)(2,1)} %copy-done.40, bf16[512,768]{1,0:T(8,128)(2,1)} %copy-done.38, bf16[256,768]{1,0:T(8,128)(2,1)} %copy-done.41, ...), custom_call_target="tpu_custom_call" | custom-call | flops 2359296 | bytes 2359296 | tf_op jit(solution)/shard_map/weight_grad/pallas_call | solution.py:328
  305.6 9.0 %collective-permute-done.47 = bf16[4,64,1152]{2,1,0:T(8,128)(2,1)S(1)} collective-permute-done((bf16[4,64,1152]{2,1,0:T(8,128)(2,1)}, bf16[4,64,1152]{2,1,0:T(8,128)(2,1)S(1)}, u32[]{:S(2)}, u32[]{:S(2)}) %collective-permute-start.47) | collective-permute-done | bytes 589856 | tf_op jit(solution)/shard_map/ppermute | solution.py:393
  327.1 4.4 %collective-permute-start.53 = (bf16[64,1152]{1,0:T(8,128)(2,1)S(1)}, bf16[64,1152]{1,0:T(8,128)(2,1)S(1)}, u32[]{:S(2)}, u32[]{:S(2)}) collective-permute-start(bf16[64,1152]{1,0:T(8,128)(2,1)S(1)} %get-tuple-element.241), channel_id=1, source_target_pairs={{0,64},{32,96},{64,0},{96,32},{1,65},{33,97},{65,1},{97,33},{2,66}... | collective-permute-start | bytes 442376 | tf_op jit(solution)/shard_map/ppermute | solution.py:393
  337.0 6.8 %all-to-all-start.1 = ((bf16[8,16,3072]{2,1,0:T(8,128)(2,1)}), bf16[8,16,3072]{2,1,0:T(8,128)(2,1)S(1)}, u32[]{:S(2)}, u32[]{:S(2)}) async-start(bf16[8,16,3072]{2,1,0:T(8,128)(2,1)} %bitcast.237), calls=%async_computation.3 | async-start | bytes 1572864 | tf_op jit(solution)/shard_map/all_to_all | solution.py:753
  349.9 13.3 %collective-permute-done.54 = bf16[16,2176]{1,0:T(8,128)(2,1)S(1)} collective-permute-done((bf16[16,2176]{1,0:T(8,128)(2,1)S(1)}, bf16[16,2176]{1,0:T(8,128)(2,1)S(1)}, u32[]{:S(2)}, u32[]{:S(2)}) %collective-permute-start.54) | collective-permute-done | bytes 69664 | tf_op jit(solution)/shard_map/ppermute | solution.py:748
  (431 shorter events, 187.7 us)
Async XLA Ops:
  7.2 75.3 %all-gather.3.cloned.1.call-start = ((), (), s32[]{:S(2)}) async-start(), calls=%async_computation.4 | async-start | bytes 9437184 | tf_op jit(solution)/shard_map/all_gather | solution.py:577
  13.4 20.6 %all-to-all-start = ((bf16[8,16,3008]{2,1,0:T(8,128)(2,1)}), bf16[8,16,3008]{2,1,0:T(8,128)(2,1)S(1)}, u32[]{:S(2)}, u32[]{:S(2)}) async-start(bf16[8,16,3008]{2,1,0:T(8,128)(2,1)} %pad_maximum_fusion.8), calls=%async_computation | async-start | bytes 1572864 | tf_op jit(solution)/shard_map/all_to_all | solution.py:590
  18.2 126.6 %all-gather.5.cloned.1.call-start = ((), (), s32[]{:S(2)}) async-start(), calls=%async_computation.5 | async-start | bytes 9469952 | tf_op jit(solution)/shard_map/all_gather | solution.py:593
  18.2 18.0 %collective-permute-start = (bf16[16,2048]{1,0:T(8,128)(2,1)S(1)}, bf16[16,2048]{1,0:T(8,128)(2,1)S(1)}, u32[]{:S(2)}, u32[]{:S(2)}) collective-permute-start(bf16[16,2048]{1,0:T(8,128)(2,1)S(1)} %slice.325), channel_id=1, source_target_pairs={{0,0},{16,1},{32,2},{48,3},{64,4},{80,5},{96,6},{112,7},{1,8},{17,... | collective-permute-start | bytes 196616 | tf_op jit(solution)/shard_map/ppermute | solution.py:591
  34.9 285.3 %reduce-scatter.5.cloned.1.call-start = ((), (), s32[]{:S(2)}) async-start(), calls=%async_computation.7 | async-start | bytes 9469952 | tf_op jit(solution)/shard_map/reduce_scatter | solution.py:672
  48.5 16.8 %collective-permute-start.4 = (bf16[4,64,1152]{2,1,0:T(8,128)(2,1)S(1)}, bf16[4,64,1152]{2,1,0:T(8,128)(2,1)S(1)}, u32[]{:S(2)}, u32[]{:S(2)}) collective-permute-start(bf16[4,64,1152]{2,1,0:T(8,128)(2,1)S(1)} %bitcast_dynamic-update-slice_fusion.14), channel_id=1, source_target_pairs={{0,32},{32,64},{64,96},{96,0},{1,33},{33,65},{65,97},{97,1},{2,34}... | collective-permute-start | bytes 1769480 | tf_op jit(solution)/shard_map/ppermute | solution.py:393
  50.1 16.8 %collective-permute-start.5 = (bf16[4,64,1152]{2,1,0:T(8,128)(2,1)S(1)}, bf16[4,64,1152]{2,1,0:T(8,128)(2,1)S(1)}, u32[]{:S(2)}, u32[]{:S(2)}) collective-permute-start(bf16[4,64,1152]{2,1,0:T(8,128)(2,1)S(1)} %bitcast_dynamic-update-slice_fusion.14), channel_id=1, source_target_pairs={{0,96},{32,0},{64,32},{96,64},{1,97},{33,1},{65,33},{97,65},{2,98}... | collective-permute-start | bytes 1769480 | tf_op jit(solution)/shard_map/ppermute | solution.py:393
  52.6 16.6 %collective-permute-start.11 = (bf16[4,64,1152]{2,1,0:T(8,128)(2,1)S(1)}, bf16[4,64,1152]{2,1,0:T(8,128)(2,1)S(1)}, u32[]{:S(2)}, u32[]{:S(2)}) collective-permute-start(bf16[4,64,1152]{2,1,0:T(8,128)(2,1)S(1)} %bitcast_dynamic-update-slice_fusion.10), channel_id=1, source_target_pairs={{0,8},{8,16},{16,24},{24,0},{1,9},{9,17},{17,25},{25,1},{2,10},{10... | collective-permute-start | bytes 1769480 | tf_op jit(solution)/shard_map/ppermute | solution.py:393
  52.8 16.4 %collective-permute-start.12 = (bf16[4,64,1152]{2,1,0:T(8,128)(2,1)S(1)}, bf16[4,64,1152]{2,1,0:T(8,128)(2,1)}, u32[]{:S(2)}, u32[]{:S(2)}) collective-permute-start(bf16[4,64,1152]{2,1,0:T(8,128)(2,1)S(1)} %bitcast_dynamic-update-slice_fusion.10), channel_id=1, source_target_pairs={{0,24},{8,0},{16,8},{24,16},{1,25},{9,1},{17,9},{25,17},{2,26},{10... | collective-permute-start | bytes 1769480 | tf_op jit(solution)/shard_map/ppermute | solution.py:393
  111.2 15.0 %collective-permute-start.18 = (bf16[256,2048]{1,0:T(8,128)(2,1)S(1)}, bf16[256,2048]{1,0:T(8,128)(2,1)S(1)}, u32[]{:S(2)}, u32[]{:S(2)}) collective-permute-start(bf16[256,2048]{1,0:T(8,128)(2,1)S(1)} %pad_maximum_fusion.5), channel_id=1, source_target_pairs={{0,6},{1,3},{2,0},{3,5},{4,2},{5,7},{6,4},{7,1},{8,14},{9,11},{10,... | collective-permute-start | bytes 3145736 | tf_op jit(solution)/shard_map/ppermute | solution.py:418
  132.5 22.2 %collective-permute-start.21 = (bf16[256,2048]{1,0:T(8,128)(2,1)}, bf16[256,2048]{1,0:T(8,128)(2,1)}, u32[]{:S(2)}, u32[]{:S(2)}) collective-permute-start(bf16[256,2048]{1,0:T(8,128)(2,1)} %join_rows.2.refs_0_), channel_id=1, source_target_pairs={{0,2},{1,7},{2,4},{3,1},{4,6},{5,3},{6,0},{7,5},{8,10},{9,15},{10,... | collective-permute-start | bytes 3145736 | tf_op jit(solution)/shard_map/ppermute | solution.py:418
  188.6 15.1 %collective-permute-start.28 = (bf16[256,2048]{1,0:T(8,128)(2,1)}, bf16[256,2048]{1,0:T(8,128)(2,1)}, u32[]{:S(2)}, u32[]{:S(2)}) collective-permute-start(bf16[256,2048]{1,0:T(8,128)(2,1)} %pad_maximum_fusion.6), channel_id=1, source_target_pairs={{0,6},{1,3},{2,0},{3,5},{4,2},{5,7},{6,4},{7,1},{8,14},{9,11},{10,... | collective-permute-start | bytes 3145736 | tf_op jit(solution)/shard_map/ppermute | solution.py:418
  203.4 131.4 %reduce-scatter.3.cloned.1.call-start = ((), (), s32[]{:S(2)}) async-start(), calls=%async_computation.6 | async-start | bytes 4718592 | tf_op jit(solution)/shard_map/reduce_scatter | solution.py:729
  215.8 17.8 %collective-permute-start.36 = (bf16[256,2048]{1,0:T(8,128)(2,1)S(1)}, bf16[256,2048]{1,0:T(8,128)(2,1)S(1)}, u32[]{:S(2)}, u32[]{:S(2)}) collective-permute-start(bf16[256,2048]{1,0:T(8,128)(2,1)S(1)} %slice.360), channel_id=1, source_target_pairs={{0,1},{1,0},{2,3},{3,2},{4,5},{5,4},{6,7},{7,6},{8,9},{9,8},{10,11... | collective-permute-start | bytes 3145736 | tf_op jit(solution)/shard_map/ppermute | solution.py:397
  217.6 15.4 %collective-permute-start.31 = (bf16[256,2048]{1,0:T(8,128)(2,1)S(1)}, bf16[256,2048]{1,0:T(8,128)(2,1)S(1)}, u32[]{:S(2)}, u32[]{:S(2)}) collective-permute-start(bf16[256,2048]{1,0:T(8,128)(2,1)S(1)} %join_rows.3), channel_id=1, source_target_pairs={{0,2},{1,7},{2,4},{3,1},{4,6},{5,3},{6,0},{7,5},{8,10},{9,15},{10,... | collective-permute-start | bytes 3145736 | tf_op jit(solution)/shard_map/ppermute | solution.py:418
  235.8 17.9 %collective-permute-start.34 = (bf16[128,2048]{1,0:T(8,128)(2,1)S(1)}, bf16[128,2048]{1,0:T(8,128)(2,1)S(1)}, u32[]{:S(2)}, u32[]{:S(2)}) collective-permute-start(bf16[128,2048]{1,0:T(8,128)(2,1)S(1)} %get-tuple-element.132.refs_0_.refs_5_), channel_id=1, source_target_pairs={{0,2},{1,7},{2,4},{3,1},{4,6},{5,3},{6,0},{7,5},{8,10},{9,15},{10,... | collective-permute-start | bytes 1572872 | tf_op jit(solution)/shard_map/ppermute | solution.py:418
  236.6 17.2 %collective-permute-start.37 = (bf16[128,2048]{1,0:T(8,128)(2,1)S(1)}, bf16[128,2048]{1,0:T(8,128)(2,1)S(1)}, u32[]{:S(2)}, u32[]{:S(2)}) collective-permute-start(bf16[128,2048]{1,0:T(8,128)(2,1)S(1)} %add_convert_fusion.1), channel_id=1, source_target_pairs={{0,6},{1,3},{2,0},{3,5},{4,2},{5,7},{6,4},{7,1},{8,14},{9,11},{10,... | collective-permute-start | bytes 1572872 | tf_op jit(solution)/shard_map/ppermute | solution.py:418
  255.0 17.1 %collective-permute-start.38 = (bf16[256,2048]{1,0:T(8,128)(2,1)}, bf16[256,2048]{1,0:T(8,128)(2,1)}, u32[]{:S(2)}, u32[]{:S(2)}) collective-permute-start(bf16[256,2048]{1,0:T(8,128)(2,1)} %pad_maximum_fusion.7), channel_id=1, source_target_pairs={{0,6},{1,3},{2,0},{3,5},{4,2},{5,7},{6,4},{7,1},{8,14},{9,11},{10,... | collective-permute-start | bytes 3145736 | tf_op jit(solution)/shard_map/ppermute | solution.py:418
  298.6 16.0 %collective-permute-start.47 = (bf16[4,64,1152]{2,1,0:T(8,128)(2,1)}, bf16[4,64,1152]{2,1,0:T(8,128)(2,1)S(1)}, u32[]{:S(2)}, u32[]{:S(2)}) collective-permute-start(bf16[4,64,1152]{2,1,0:T(8,128)(2,1)} %fusion.36), channel_id=1, source_target_pairs={{0,24},{8,0},{16,8},{24,16},{1,25},{9,1},{17,9},{25,17},{2,26},{10... | collective-permute-start | bytes 1769480 | tf_op jit(solution)/shard_map/ppermute | solution.py:393
  300.7 16.8 %collective-permute-start.46 = (bf16[4,64,1152]{2,1,0:T(8,128)(2,1)}, bf16[4,64,1152]{2,1,0:T(8,128)(2,1)S(1)}, u32[]{:S(2)}, u32[]{:S(2)}) collective-permute-start(bf16[4,64,1152]{2,1,0:T(8,128)(2,1)} %fusion.35), channel_id=1, source_target_pairs={{0,8},{8,16},{16,24},{24,0},{1,9},{9,17},{17,25},{25,1},{2,10},{10... | collective-permute-start | bytes 1769480 | tf_op jit(solution)/shard_map/ppermute | solution.py:393
  300.7 18.1 %collective-permute-start.45 = (bf16[4,64,1152]{2,1,0:T(8,128)(2,1)}, bf16[4,64,1152]{2,1,0:T(8,128)(2,1)S(1)}, u32[]{:S(2)}, u32[]{:S(2)}) collective-permute-start(bf16[4,64,1152]{2,1,0:T(8,128)(2,1)} %copy-done.65), channel_id=1, source_target_pairs={{0,96},{32,0},{64,32},{96,64},{1,97},{33,1},{65,33},{97,65},{2,98}... | collective-permute-start | bytes 1769480 | tf_op jit(solution)/shard_map/ppermute | solution.py:393
  302.1 16.8 %collective-permute-start.44 = (bf16[4,64,1152]{2,1,0:T(8,128)(2,1)}, bf16[4,64,1152]{2,1,0:T(8,128)(2,1)S(1)}, u32[]{:S(2)}, u32[]{:S(2)}) collective-permute-start(bf16[4,64,1152]{2,1,0:T(8,128)(2,1)} %copy-done.64), channel_id=1, source_target_pairs={{0,32},{32,64},{64,96},{96,0},{1,33},{33,65},{65,97},{97,1},{2,34}... | collective-permute-start | bytes 1769480 | tf_op jit(solution)/shard_map/ppermute | solution.py:393
  337.0 27.1 %all-to-all-start.1 = ((bf16[8,16,3072]{2,1,0:T(8,128)(2,1)}), bf16[8,16,3072]{2,1,0:T(8,128)(2,1)S(1)}, u32[]{:S(2)}, u32[]{:S(2)}) async-start(bf16[8,16,3072]{2,1,0:T(8,128)(2,1)} %bitcast.237), calls=%async_computation.3 | async-start | bytes 1572864 | tf_op jit(solution)/shard_map/all_to_all | solution.py:753
  343.9 19.3 %collective-permute-start.54 = (bf16[16,2176]{1,0:T(8,128)(2,1)S(1)}, bf16[16,2176]{1,0:T(8,128)(2,1)S(1)}, u32[]{:S(2)}, u32[]{:S(2)}) collective-permute-start(bf16[16,2176]{1,0:T(8,128)(2,1)S(1)} %pad_maximum_fusion.14), channel_id=1, source_target_pairs={{0,0},{1,16},{2,32},{3,48},{4,64},{5,80},{6,96},{7,112},{8,1},{9,1... | collective-permute-start | bytes 208904 | tf_op jit(solution)/shard_map/ppermute | solution.py:748
  (114 other events, 654.1 us)
Sparse Core Ops, SparseCore 0:
  10.3 54.8 all-gather.2
  67.9 76.8 all-gather.4
  203.6 85.7 reduce-scatter.4
  296.3 37.6 reduce-scatter.2
